TPU v7x, 512 devices: a whole 4x4x16 slice. The times are simulated.
512 devices in a mesh: scene: 8 (over y, core), brick: 64 (over x, z).
Axes of the slice: x: 4, y: 4, z: 16, core: 2. Of those that a mesh axis runs over, the one named last changes fastest.
Arguments:
- tokens: bfloat16 [524288, 384], P(('scene', 'brick')), parts along dimension 0, may hold values from -6 to 6
- token_voxel: int32 [524288], P(('scene', 'brick')), parts along dimension 0, may hold values from 0 to 32767, as said below
- in_weight: bfloat16 [384, 128], replicated, may hold values from -0.3125 to 0.3125
- conv_weight: bfloat16 [27, 128, 128], replicated, may hold values from -0.109375 to 0.109375
- channel_gain: float32 [128], replicated, may hold values from 0.5 to 1.5
- rule_in: int32 [512, 27, 512], P(('scene', 'brick')), parts along dimension 0, may hold values from 0 to 511
- rule_out: int32 [512, 27, 512], P(('scene', 'brick')), parts along dimension 0, may hold values from 0 to 640, as said below
- halo_slots: int32 [512, 2, 64], P(('scene', 'brick')), parts along dimension 0, may hold values from 0 to 511
Outputs:
- voxel_out: bfloat16 [262144, 128], P(('scene', 'brick')), parts along dimension 0
There are 8 independent parts, one for each index of `scene`. A program takes and returns all parts, laid end to end along the dimension named above; an argument that names none is the same for every part. Nothing has to cross between parts.
Inputs may be any that keep to these rules, and one draw needn't show every extreme that they name: `token_voxel`: voxel v belongs to owner v // 512 at slot v % 512. Of one device's tokens at most 32 go to one owner, and on every device some owner gets exactly 32. `rule_out`: below 512: an own voxel slot. 512 + e: row e of the partial outputs for the lower neighbour; 576 + e: row e for the upper neighbour; 640: a padding pair. The first device names no lower rows, the last no upper ones. halo_slots[j, 0, e] receives row e of the lower neighbour's upper partial outputs, halo_slots[j, 1, e] row e of the upper neighbour's lower ones.
All inputs are finite; a program needn't handle non-finite values.
Results may differ from a plain program's by a relative error of at most 0.0052.
Values may be sent and summed in bfloat16 or wider, within the bound.
No kernel may reach another device: no remote copies, remote signals or barrier semaphores. Data moves between devices by JAX's collectives and lax.ppermute only.
A program may use at most 64 MiB of HBM per device.

v0:
```python
import jax
import jax.numpy as jnp
from jax import lax
from jax.sharding import PartitionSpec as P

VOX_DEV = 512


def passed_along(block, axis, distance):
    devices = range(lax.axis_size(axis))
    route = [(i - distance, i) for i in devices if i - distance in devices]
    return lax.ppermute(block, axis, route)


def per_device(
    tokens, token_voxel, in_weight, conv_weight, channel_gain, rule_in, rule_out, halo_slots
):
    highest = lax.Precision.HIGHEST
    bricks = lax.axis_size("brick")
    tok_count = tokens.shape[0]
    capacity = 2 * tok_count // bricks
    edge_rows = halo_slots.shape[2]
    width = in_weight.shape[1]
    owner_dev = token_voxel // VOX_DEV
    local_slot = token_voxel % VOX_DEV
    member = (owner_dev[:, None] == jnp.arange(bricks, dtype=jnp.int32)[None, :]).astype(
        jnp.bfloat16
    )
    tok_index = jnp.arange(tok_count, dtype=jnp.int32)
    lower_tri = (tok_index[:, None] >= tok_index[None, :]).astype(jnp.bfloat16)
    running = jnp.dot(lower_tri, member, preferred_element_type=jnp.float32)
    slot_rank = jnp.sum(running * member.astype(jnp.float32), axis=1).astype(jnp.int32) - 1
    position = owner_dev * capacity + slot_rank
    send_index = jnp.arange(bricks * capacity, dtype=jnp.int32)
    pack_table = send_index[:, None] == position[None, :]
    pack_bf = pack_table.astype(jnp.bfloat16)
    slot_plus = jnp.dot(
        pack_table.astype(jnp.float32), (local_slot + 1).astype(jnp.float32), precision=highest
    )
    slot_value = slot_plus.astype(jnp.int32) - 1
    send_slots = jnp.where(slot_value < 0, VOX_DEV, slot_value)
    got_slots = lax.all_to_all(
        send_slots.reshape(bricks, capacity), "brick", split_axis=0, concat_axis=0, tiled=True
    ).reshape(-1)
    packed = jnp.dot(pack_bf, tokens, preferred_element_type=jnp.float32).astype(jnp.bfloat16)
    arrived = lax.all_to_all(
        packed.reshape(bricks, capacity, tokens.shape[1]),
        "brick",
        split_axis=0,
        concat_axis=0,
        tiled=True,
    )
    arrived_proj = jnp.dot(
        arrived.reshape(bricks * capacity, tokens.shape[1]),
        in_weight,
        preferred_element_type=jnp.float32,
    ).astype(jnp.bfloat16)
    vox_index = jnp.arange(VOX_DEV, dtype=jnp.int32)
    seg_table = vox_index[:, None] == got_slots[None, :]
    voxel_sums = jnp.dot(
        seg_table.astype(jnp.bfloat16), arrived_proj, preferred_element_type=jnp.float32
    )
    counts = jnp.sum(seg_table.astype(jnp.float32), axis=1)
    voxels = (voxel_sums / jnp.maximum(counts, 1.0)[:, None]).astype(jnp.bfloat16)
    combined = VOX_DEV + 2 * edge_rows + 1
    row_index = jnp.arange(combined, dtype=jnp.int32)

    def offset_step(totals, offset_items):
        weight, source, target = offset_items
        pick = (source[:, None] == vox_index[None, :]).astype(jnp.bfloat16)
        gathered = jnp.dot(pick, voxels, preferred_element_type=jnp.float32).astype(jnp.bfloat16)
        products = jnp.dot(gathered, weight, preferred_element_type=jnp.float32)
        place = (row_index[:, None] == target[None, :]).astype(jnp.float32)
        return (totals + jnp.dot(place, products, precision=highest), None)

    start = jnp.zeros((combined, width), jnp.float32)
    totals = lax.scan(offset_step, start, (conv_weight, rule_in[0], rule_out[0]))[0]
    to_lower = totals[VOX_DEV : VOX_DEV + edge_rows]
    to_upper = totals[VOX_DEV + edge_rows : VOX_DEV + 2 * edge_rows]
    from_lower = passed_along(to_upper.astype(jnp.bfloat16), "brick", 1).astype(to_upper.dtype)
    from_upper = passed_along(to_lower.astype(jnp.bfloat16), "brick", -1).astype(to_lower.dtype)
    lower_place = (vox_index[:, None] == halo_slots[0, 0][None, :]).astype(jnp.float32)
    upper_place = (vox_index[:, None] == halo_slots[0, 1][None, :]).astype(jnp.float32)
    conv_sum = (
        totals[:VOX_DEV]
        + jnp.dot(lower_place, from_lower, precision=highest)
        + jnp.dot(upper_place, from_upper, precision=highest)
    )
    inv_rms = lax.rsqrt(jnp.mean(conv_sum * conv_sum, axis=1, keepdims=True) + 1e-05)
    return (voxels.astype(jnp.float32) + jax.nn.relu(conv_sum * inv_rms * channel_gain)).astype(
        jnp.bfloat16
    )


def solution(mesh):
    return jax.shard_map(
        per_device,
        mesh=mesh,
        in_specs=(
            P(("scene", "brick"), None),
            P(("scene", "brick")),
            P(),
            P(),
            P(),
            P(("scene", "brick"), None, None),
            P(("scene", "brick"), None, None),
            P(("scene", "brick"), None, None),
        ),
        out_specs=P(("scene", "brick"), None),
        check_vma=False,
    )
```

profile of v0, /device:TPU:6, one launch (start us, length us, event | category | flops | bytes accessed | tf_op | source)
XLA Modules:
  0.0 188.5 jit_solution(5064591388760757120)
XLA Ops:
  1.4 3.7 %fusion.14 = f32[1,2048]{1,0:T(1,128)S(1)} fusion(f32[1024,1]{0,1:T(1,128)S(1)} %bitcast.40, s32[1024]{0:T(1024)S(1)} %get-tuple-element.90), kind=kOutput, calls=%fused_computation.17 | convolution fusion | flops 27262976 | bytes 16384 | tf_op jit(solution)/shard_map/dot_general | solution.py:37
  5.9 18.8 %all-to-all-start = ((s32[64,1,32]{2,1,0:T(1,128)}), s32[64,1,32]{2,1,0:T(1,128)S(1)}, u32[]{:S(2)}, u32[]{:S(2)}) async-start(s32[64,1,32]{2,1,0:T(1,128)} %bitcast.2), calls=%async_computation | async-start | bytes 65536 | tf_op jit(solution)/shard_map/all_to_all | solution.py:42
  24.7 3.5 %fusion.19 = bf16[2048,384]{1,0:T(8,128)(2,1)} fusion(bf16[1024,384]{1,0:T(8,128)(2,1)S(1)} %copy-done, s32[1024]{0:T(1024)S(1)} %get-tuple-element.90), kind=kOutput, calls=%fused_computation.25 | convolution fusion | flops 1613496320 | bytes 2363392 | tf_op jit(solution)/shard_map/dot_general | solution.py:45
  28.2 9.0 %all-to-all-done = s32[64,1,32]{2,1,0:T(1,128)S(1)} async-done(((s32[64,1,32]{2,1,0:T(1,128)}), s32[64,1,32]{2,1,0:T(1,128)S(1)}, u32[]{:S(2)}, u32[]{:S(2)}) %all-to-all-start) | async-done | bytes 8224 | tf_op jit(solution)/shard_map/all_to_all | solution.py:42
  37.2 6.7 %all-to-all-start.1 = ((bf16[64,32,384]{2,1,0:T(8,128)(2,1)}), bf16[64,32,384]{2,1,0:T(8,128)(2,1)S(1)}, u32[]{:S(2)}, u32[]{:S(2)}) async-start(bf16[64,32,384]{2,1,0:T(8,128)(2,1)} %bitcast.3), calls=%async_computation.1 | async-start | bytes 3145728 | tf_op jit(solution)/shard_map/all_to_all | solution.py:46
  45.8 73.3 %all-to-all-done.1 = bf16[64,32,384]{2,1,0:T(8,128)(2,1)S(1)} async-done(((bf16[64,32,384]{2,1,0:T(8,128)(2,1)}), bf16[64,32,384]{2,1,0:T(8,128)(2,1)S(1)}, u32[]{:S(2)}, u32[]{:S(2)}) %all-to-all-start.1) | async-done | bytes 1572896 | tf_op jit(solution)/shard_map/all_to_all | solution.py:46
  119.1 1.8 fusion.24
  121.0 56.7 %while.11 = (s32[]{:T(128)}, f32[641,128]{1,0:T(8,128)S(1)}, s32[27,512]{1,0:T(8,128)S(1)}, s32[27,512]{1,0:T(8,128)S(1)}, bf16[512,128]{1,0:T(8,128)(2,1)S(1)},...) while((s32[]{:T(128)}, f32[641,128]{1,0:T(8,128)S(1)}, s32[27,512]{1,0:T(8,128)S(1)}, ...), condition=%wide.region_3.4_spmd.clone, body=%wide.region_2.3_spmd.clone.sunk | while | flops 588808960 | bytes 1357411 | solution.py:77
  121.0 1.2 fusion.52
  122.2 0.8 fusion.53
  123.1 1.2 fusion.52
  125.2 1.2 fusion.52
  127.3 1.2 fusion.52
  128.5 0.8 fusion.53
  129.4 1.2 fusion.52
  131.5 1.2 fusion.52
  132.7 0.8 fusion.53
  133.6 1.2 fusion.52
  135.7 1.2 fusion.52
  137.8 1.2 fusion.52
  139.0 0.8 fusion.53
  139.9 1.2 fusion.52
  142.0 1.2 fusion.52
  143.2 0.8 fusion.53
  144.1 1.2 fusion.52
  146.2 1.2 fusion.52
  148.3 1.2 fusion.52
  149.5 0.8 fusion.53
  150.4 1.2 fusion.52
  152.5 1.2 fusion.52
  153.7 0.8 fusion.53
  154.6 1.2 fusion.52
  156.7 1.2 fusion.52
  158.8 1.2 fusion.52
  160.0 0.8 fusion.53
  160.9 1.2 fusion.52
  163.0 1.2 fusion.52
  164.2 0.8 fusion.53
  165.1 1.2 fusion.52
  167.2 1.2 fusion.52
  169.3 1.2 fusion.52
  171.4 1.2 fusion.52
  173.5 1.2 fusion.52
  174.8 0.8 fusion.53
  175.6 1.2 fusion.52
  177.7 1.9 %collective-permute-start.1 = (bf16[64,128]{1,0:T(8,128)(2,1)S(1)}, bf16[64,128]{1,0:T(8,128)(2,1)S(1)}, u32[]{:S(2)}, u32[]{:S(2)}) collective-permute-start(bf16[64,128]{1,0:T(8,128)(2,1)S(1)} %get-tuple-element.88), channel_id=1, source_target_pairs={{1,0},{2,1},{3,2},{4,3},{5,4},{6,5},{7,6},{8,7},{9,8},{10,9},{11,1... | collective-permute-start | bytes 49160 | tf_op jit(solution)/shard_map/ppermute | solution.py:12
  179.7 3.9 %collective-permute-start = (bf16[64,128]{1,0:T(8,128)(2,1)S(1)}, bf16[64,128]{1,0:T(8,128)(2,1)S(1)}, u32[]{:S(2)}, u32[]{:S(2)}) collective-permute-start(bf16[64,128]{1,0:T(8,128)(2,1)S(1)} %get-tuple-element.87), channel_id=1, source_target_pairs={{0,1},{1,2},{2,3},{3,4},{4,5},{5,6},{6,7},{7,8},{8,9},{9,10},{10,1... | collective-permute-start | bytes 49160 | tf_op jit(solution)/shard_map/ppermute | solution.py:12
  183.8 3.6 %collective-permute-done = bf16[64,128]{1,0:T(8,128)(2,1)S(1)} collective-permute-done((bf16[64,128]{1,0:T(8,128)(2,1)S(1)}, bf16[64,128]{1,0:T(8,128)(2,1)S(1)}, u32[]{:S(2)}, u32[]{:S(2)}) %collective-permute-start) | collective-permute-done | bytes 16416 | tf_op jit(solution)/shard_map/ppermute | solution.py:12
  (78 shorter events, 19.7 us)
Async XLA Ops:
  0.0 24.7 %copy-start = (bf16[1024,384]{1,0:T(8,128)(2,1)S(1)}, bf16[1024,384]{1,0:T(8,128)(2,1)}, u32[]{:S(2)}) copy-start(bf16[1024,384]{1,0:T(8,128)(2,1)} %param.10) | copy-start | bytes 2359300
  0.0 1.4 copy-start.3
  5.9 31.3 %all-to-all-start = ((s32[64,1,32]{2,1,0:T(1,128)}), s32[64,1,32]{2,1,0:T(1,128)S(1)}, u32[]{:S(2)}, u32[]{:S(2)}) async-start(s32[64,1,32]{2,1,0:T(1,128)} %bitcast.2), calls=%async_computation | async-start | bytes 65536 | tf_op jit(solution)/shard_map/all_to_all | solution.py:42
  37.2 6.7 %copy-start.1 = (s32[1,27,512]{2,0,1:T(1,128)S(1)}, s32[1,27,512]{2,0,1:T(1,128)}, u32[]{:S(2)}) copy-start(s32[1,27,512]{2,0,1:T(1,128)} %param.15) | copy-start | bytes 165892
  37.2 6.7 %copy-start.2 = (s32[1,27,512]{2,0,1:T(1,128)S(1)}, s32[1,27,512]{2,0,1:T(1,128)}, u32[]{:S(2)}) copy-start(s32[1,27,512]{2,0,1:T(1,128)} %param.16) | copy-start | bytes 165892
  37.2 82.0 %copy-start.6 = (bf16[384,128]{1,0:T(8,128)(2,1)S(1)}, bf16[384,128]{1,0:T(8,128)(2,1)}, u32[]{:S(2)}) copy-start(bf16[384,128]{1,0:T(8,128)(2,1)} %param.12) | copy-start | bytes 294916
  37.2 82.0 %all-to-all-start.1 = ((bf16[64,32,384]{2,1,0:T(8,128)(2,1)}), bf16[64,32,384]{2,1,0:T(8,128)(2,1)S(1)}, u32[]{:S(2)}, u32[]{:S(2)}) async-start(bf16[64,32,384]{2,1,0:T(8,128)(2,1)} %bitcast.3), calls=%async_computation.1 | async-start | bytes 3145728 | tf_op jit(solution)/shard_map/all_to_all | solution.py:46
  121.0 58.7 %copy-start.4 = (s32[1,2,64]{2,1,0:T(2,128)S(1)}, s32[1,2,64]{2,1,0:T(2,128)}, u32[]{:S(2)}) copy-start(s32[1,2,64]{2,1,0:T(2,128)} %param.17) | copy-start | bytes 1540
  177.7 10.0 %copy-start.5 = (f32[128]{0:T(128)S(1)}, f32[128]{0:T(128)}, u32[]{:S(2)}) copy-start(f32[128]{0:T(128)} %param.14) | copy-start | bytes 1540
  177.7 5.9 %collective-permute-start.1 = (bf16[64,128]{1,0:T(8,128)(2,1)S(1)}, bf16[64,128]{1,0:T(8,128)(2,1)S(1)}, u32[]{:S(2)}, u32[]{:S(2)}) collective-permute-start(bf16[64,128]{1,0:T(8,128)(2,1)S(1)} %get-tuple-element.88), channel_id=1, source_target_pairs={{1,0},{2,1},{3,2},{4,3},{5,4},{6,5},{7,6},{8,7},{9,8},{10,9},{11,1... | collective-permute-start | bytes 49160 | tf_op jit(solution)/shard_map/ppermute | solution.py:12
  179.7 7.7 %collective-permute-start = (bf16[64,128]{1,0:T(8,128)(2,1)S(1)}, bf16[64,128]{1,0:T(8,128)(2,1)S(1)}, u32[]{:S(2)}, u32[]{:S(2)}) collective-permute-start(bf16[64,128]{1,0:T(8,128)(2,1)S(1)} %get-tuple-element.87), channel_id=1, source_target_pairs={{0,1},{1,2},{2,3},{3,4},{4,5},{5,6},{6,7},{7,8},{8,9},{9,10},{10,1... | collective-permute-start | bytes 49160 | tf_op jit(solution)/shard_map/ppermute | solution.py:12
where the time goes:
time: 191 us; the launch traced here: 189 us
  waiting for transfers between devices  85.9 us (45%)
  matrix products  65.7 us (34%)
  starting transfers between devices  31.3 us (16%)
  other arithmetic  2.89 us (2%)
    all_to_all x1, waiting for transfers between devices, per_device(): lax.all_to_all(packed.reshape(bricks, capacity, tokens.shape[1]), 'brick'...  73.3 us
    dot_general x27, matrix products, offset_step(): products = jnp.dot(gathered, weight, preferred_element_type=jnp.float32)  33.2 us
    dot_general x27, matrix products, offset_step(): return (totals + jnp.dot(place, products, precision=highest), None)  22.3 us
    all_to_all x1, starting transfers between devices, per_device(): lax.all_to_all(send_slots.reshape(bricks, capacity), 'brick', split_axis=...  18.8 us
    all_to_all x1, waiting for transfers between devices, per_device(): lax.all_to_all(send_slots.reshape(bricks, capacity), 'brick', split_axis=...  8.97 us
    all_to_all x1, starting transfers between devices, per_device(): lax.all_to_all(packed.reshape(bricks, capacity, tokens.shape[1]), 'brick'...  6.68 us
    ppermute x2, starting transfers between devices, passed_along(): return lax.ppermute(block, axis, route)  5.84 us
  transfers between devices with their start and end apart: 4, of which 3 were waited for; matrix products, arithmetic and copies ran while one was open for 3% of the time, Pallas kernels for 0%

commit v1 on v0

v1 whole, which is shorter than its diff:
```python
import functools

import jax
import jax.numpy as jnp
import numpy as np
from jax import lax
from jax.experimental import pallas as pl
from jax.experimental.pallas import tpu as pltpu
from jax.sharding import PartitionSpec as P

VOX = 512
LANES = 128
BF = jnp.bfloat16
F32 = jnp.float32
VMEM_LIMIT = 50 * 1024 * 1024


def passed_along(block, axis, distance):
    devices = range(lax.axis_size(axis))
    route = [(i - distance, i) for i in devices if i - distance in devices]
    return lax.ppermute(block, axis, route)


def dot(a, b):
    return jnp.dot(a, b, preferred_element_type=F32)


def dot_t(a, b):
    return lax.dot_general(a, b, (((1,), (1,)), ((), ())), preferred_element_type=F32)


def row_iota(rows):
    return lax.broadcasted_iota(jnp.int32, (rows, LANES), 0).astype(F32).astype(BF)


def one_hot_rows(numbers, value, start):
    rows = numbers.shape[0]
    here = jnp.clip(value - start, -1, rows).astype(F32).astype(BF)
    return jnp.where(
        numbers == jnp.broadcast_to(here, numbers.shape), jnp.ones_like(numbers), jnp.zeros_like(numbers)
    )


def prep_kernel(bricks, cap, me_ref, voxel_ref, tokens_ref, weight_ref, extra_ref, out_ref):
    per = cap + 2
    rows = bricks * per
    chunks = voxel_ref.shape[0]
    projected = dot(tokens_ref[...], weight_ref[...]).astype(BF)
    t_from = lax.broadcasted_iota(jnp.int32, (LANES, LANES), 0)
    t_to = lax.broadcasted_iota(jnp.int32, (LANES, LANES), 1)
    upper = jnp.where(t_from <= t_to, 1.0, 0.0).astype(BF)
    brick_id = lax.broadcasted_iota(jnp.int32, (bricks, LANES), 0)
    owners = [voxel_ref[b : b + 1, :] // VOX for b in range(chunks)]
    slots = [voxel_ref[b : b + 1, :] % VOX for b in range(chunks)]
    member = [jnp.where(brick_id == o, 1.0, 0.0) for o in owners]
    running = dot(jnp.concatenate(member, axis=0).astype(BF), upper)
    before = jnp.zeros((bricks, 1), F32)
    shift = me_ref[0] * per
    lane_id = lax.broadcasted_iota(jnp.int32, (LANES, LANES), 0)
    position, slot_cols = [], []
    for b in range(chunks):
        run = running[b * bricks : (b + 1) * bricks]
        rank = jnp.sum(member[b] * (run + before), axis=0, keepdims=True).astype(jnp.int32) - 1
        before = before + run[:, LANES - 1 :]
        position.append(owners[b] * per + rank)
        at = lane_id == (rank + shift) % LANES
        plus = slots[b] + 1
        low = jnp.where(at, (plus % 256).astype(F32), 0.0)
        high = jnp.where(at, (plus // 256).astype(F32), 0.0)
        slot_cols.append(jnp.concatenate([low, high], axis=0).astype(BF))
    slot_rows = dot_t(
        jnp.concatenate(member, axis=1).astype(BF), jnp.concatenate(slot_cols, axis=1)
    ).astype(BF)
    source = jnp.concatenate([projected, slot_rows[:, :LANES], slot_rows[:, LANES:]], axis=0)
    position.append(extra_ref[...])
    size = 256
    for start in range(0, rows, size):
        n = min(size, rows - start)
        numbers = row_iota(n)
        table = jnp.concatenate([one_hot_rows(numbers, p, start) for p in position], axis=1)
        out_ref[start : start + n, :] = dot(table, source).astype(BF)


def rules_kernel(rule_in_ref, rule_out_ref, own_ref, edge_ref):
    k = pl.program_id(0)
    pairs = rule_in_ref.shape[1]
    source = rule_in_ref[pl.ds(k, 1), :]
    target = rule_out_ref[pl.ds(k, 1), :]
    numbers = row_iota(256)

    def table(value, start, n):
        return jnp.concatenate(
            [
                one_hot_rows(numbers[:n], value[:, c : c + LANES], start)
                for c in range(0, pairs, LANES)
            ],
            axis=1,
        )

    pick = jnp.concatenate([table(source, s, 256) for s in range(0, VOX, 256)], axis=0)
    for s in range(0, VOX, 256):
        own_ref[0, s : s + 256, :] = dot_t(table(target, s, 256), pick).astype(BF)
    edge_ref[0] = dot_t(table(target, VOX, edge_ref.shape[1]), pick).astype(BF)


def mix(counts, voxels, weights):
    width = voxels.shape[1]
    offsets = weights.shape[0] // width
    rows = counts.shape[0] // offsets
    gathered = dot(counts, voxels).astype(BF)
    side = jnp.concatenate([gathered[k * rows : (k + 1) * rows] for k in range(offsets)], axis=1)
    return dot(side, weights)


def voxel_kernel(bricks, cap, arrived_ref, class_ref, edge_counts_ref, conv_ref, voxels_ref, lower_ref, upper_ref):
    per = cap + 2
    chunks = class_ref.shape[0]
    arrived = arrived_ref[...]
    numbers = row_iota(256)
    pick = jnp.concatenate(
        [one_hot_rows(numbers[: 2 * bricks], class_ref[c : c + 1, :], 0) for c in range(chunks)], axis=1
    )
    coded = dot(pick, arrived)
    low, high = coded[:bricks], coded[bricks:]
    begin = lax.broadcasted_iota(jnp.int32, (bricks, LANES), 0) * per
    lane = lax.broadcasted_iota(jnp.int32, (bricks, LANES), 1)
    stays = lane >= begin % LANES
    spread = jnp.concatenate(
        [
            jnp.concatenate([jnp.where(stays, x, 0.0), jnp.where(stays, 0.0, x)], axis=0)
            for x in (low, high)
        ],
        axis=1,
    ).astype(BF)
    chunk_id = lax.broadcasted_iota(jnp.int32, (32, 2 * bricks), 0)
    column = lax.broadcasted_iota(jnp.int32, (32, 2 * bricks), 1)
    wraps = jnp.where(column >= bricks, 1, 0)
    chunk_of = ((column - wraps * bricks) * per) // LANES + wraps
    lined = dot(jnp.where(chunk_id == chunk_of, 1.0, 0.0).astype(BF), spread)
    slot = (lined[:, :LANES] + 256.0 * lined[:, LANES:]).astype(jnp.int32) - 1
    right = jnp.concatenate([arrived, jnp.ones_like(arrived)], axis=1)
    parts = []
    for s in range(0, VOX, 256):
        table = jnp.concatenate(
            [one_hot_rows(numbers, slot[c : c + 1, :], s) for c in range(chunks)], axis=1
        )
        both = dot(table, right)
        parts.append((both[:, :LANES] / jnp.maximum(both[:, LANES:], 1.0)).astype(BF))
    voxels = jnp.concatenate(parts, axis=0)
    voxels_ref[...] = voxels
    edge = mix(edge_counts_ref[...], voxels, conv_ref[...]).astype(BF)
    half = lower_ref.shape[0]
    lower_ref[...] = edge[:half]
    upper_ref[...] = edge[half:]


def own_kernel(counts_ref, voxels_ref, conv_ref, out_ref):
    @pl.when(pl.program_id(0) == 0)
    def _():
        out_ref[...] = jnp.zeros_like(out_ref)

    out_ref[...] += mix(counts_ref[...], voxels_ref[...], conv_ref[...])


def final_kernel(own_ref, voxels_ref, halo_ref, from_lower_ref, from_upper_ref, gain_ref, out_ref):
    numbers = row_iota(256)
    partial = jnp.concatenate([from_lower_ref[...], from_upper_ref[...]], axis=0)
    for s in range(0, VOX, 256):
        place = one_hot_rows(numbers, halo_ref[...], s)
        conv_sum = own_ref[s : s + 256, :] + dot(place, partial)
        inv_rms = lax.rsqrt(jnp.mean(conv_sum * conv_sum, axis=1, keepdims=True) + 1e-05)
        fresh = jnp.maximum(conv_sum * inv_rms * gain_ref[...], 0.0)
        out_ref[s : s + 256, :] = (voxels_ref[s : s + 256, :].astype(F32) + fresh).astype(BF)


def params(semantics=None):
    return pltpu.CompilerParams(vmem_limit_bytes=VMEM_LIMIT, dimension_semantics=semantics)


def cost(flops, moved):
    return pl.CostEstimate(flops=int(flops), bytes_accessed=int(moved), transcendentals=0)


def per_device(
    tokens, token_voxel, in_weight, conv_weight, channel_gain, rule_in, rule_out, halo_slots
):
    bricks = lax.axis_size("brick")
    tok_count = tokens.shape[0]
    cap = 2 * tok_count // bricks
    per = cap + 2
    rows = bricks * per
    offsets, width = conv_weight.shape[0], conv_weight.shape[2]
    pairs = rule_in.shape[2]
    edges = 2 * halo_slots.shape[2]
    me = lax.axis_index("brick").astype(jnp.int32).reshape(1)
    row_number = np.arange(rows)
    brick_of, rank_of = row_number // per, row_number % per
    classes = np.where(rank_of >= cap, (rank_of - cap) * bricks + brick_of, -1)
    classes = jnp.asarray(classes.reshape(rows // LANES, LANES), jnp.int32)
    extra = np.concatenate([np.arange(bricks) * per + cap, np.arange(bricks) * per + cap + 1])
    extra = jnp.asarray(extra.reshape(1, 2 * bricks), jnp.int32)
    conv_rows = conv_weight.reshape(offsets * width, width)
    vmem = pl.BlockSpec(memory_space=pltpu.VMEM)

    send = pl.pallas_call(
        functools.partial(prep_kernel, bricks, cap),
        out_shape=jax.ShapeDtypeStruct((rows, width), BF),
        in_specs=[pl.BlockSpec(memory_space=pltpu.SMEM)] + [vmem] * 4,
        out_specs=vmem,
        compiler_params=params(),
        cost_estimate=cost(2 * rows * 1152 * width, 2_000_000),
        name="prep",
    )(me, token_voxel.reshape(tok_count // LANES, LANES), tokens, in_weight, extra)

    arrived = lax.all_to_all(
        send.reshape(bricks, per // 2, 2, width), "brick", split_axis=0, concat_axis=0, tiled=True
    ).reshape(rows, width)

    own_counts, edge_counts = pl.pallas_call(
        rules_kernel,
        out_shape=(
            jax.ShapeDtypeStruct((offsets, VOX, VOX), BF),
            jax.ShapeDtypeStruct((offsets, edges, VOX), BF),
        ),
        grid=(offsets,),
        in_specs=[pl.BlockSpec((offsets, pairs), lambda k: (0, 0))] * 2,
        out_specs=(
            pl.BlockSpec((1, VOX, VOX), lambda k: (k, 0, 0)),
            pl.BlockSpec((1, edges, VOX), lambda k: (k, 0, 0)),
        ),
        compiler_params=params(("arbitrary",)),
        cost_estimate=cost(2 * offsets * (VOX + edges) * VOX * pairs, 2 * offsets * (VOX + edges) * VOX),
        name="rules",
    )(rule_in[0], rule_out[0])

    voxels, to_lower, to_upper = pl.pallas_call(
        functools.partial(voxel_kernel, bricks, cap),
        out_shape=(
            jax.ShapeDtypeStruct((VOX, width), BF),
            jax.ShapeDtypeStruct((edges // 2, width), BF),
            jax.ShapeDtypeStruct((edges // 2, width), BF),
        ),
        in_specs=[vmem] * 4,
        out_specs=(vmem, vmem, vmem),
        compiler_params=params(),
        cost_estimate=cost(2 * offsets * edges * VOX * width, 6_000_000),
        name="voxel",
    )(arrived, classes, edge_counts.reshape(offsets * edges, VOX), conv_rows)

    from_lower = passed_along(to_upper, "brick", 1)
    from_upper = passed_along(to_lower, "brick", -1)

    group = 3
    own = pl.pallas_call(
        own_kernel,
        out_shape=jax.ShapeDtypeStruct((VOX, width), F32),
        grid=(offsets // group,),
        in_specs=[
            pl.BlockSpec((group * VOX, VOX), lambda k: (k, 0)),
            pl.BlockSpec((VOX, width), lambda k: (0, 0)),
            pl.BlockSpec((group * width, width), lambda k: (k, 0)),
        ],
        out_specs=pl.BlockSpec((VOX, width), lambda k: (0, 0)),
        compiler_params=params(("arbitrary",)),
        cost_estimate=cost(2 * offsets * VOX * (VOX + width) * width, 2 * offsets * VOX * VOX),
        name="own",
    )(own_counts.reshape(offsets * VOX, VOX), voxels, conv_rows)

    return pl.pallas_call(
        final_kernel,
        out_shape=jax.ShapeDtypeStruct((VOX, width), BF),
        in_specs=[vmem] * 6,
        out_specs=vmem,
        compiler_params=params(),
        cost_estimate=cost(2 * VOX * width * width, 1_000_000),
        name="final",
    )(own, voxels, halo_slots.reshape(1, edges), from_lower, from_upper, channel_gain.reshape(1, width))


def solution(mesh):
    return jax.shard_map(
        per_device,
        mesh=mesh,
        in_specs=(
            P(("scene", "brick"), None),
            P(("scene", "brick")),
            P(),
            P(),
            P(),
            P(("scene", "brick"), None, None),
            P(("scene", "brick"), None, None),
            P(("scene", "brick"), None, None),
        ),
        out_specs=P(("scene", "brick"), None),
        check_vma=False,
    )
```

time: 191 us -> 83.5 us (0.44)
  waiting for transfers between devices: 85.9 us -> 11.3 us
  matrix products: 65.7 us -> 0 us
  Pallas kernels: 0 us -> 38.1 us
  local copies, waits for them, and re-layouts: 1.72 us -> 6.74 us
  starting transfers between devices: 31.3 us -> 26.7 us
  other arithmetic: 2.89 us -> 0 us
    all_to_all x2 -> x1, waiting for transfers between devices: 82.3 us -> 11.2 us  [per_device(): lax.all_to_all(send.reshape(bricks, per // 2, 2, width), 'brick', split_a...]
    dot_general x60 -> x0, matrix products: 65.7 us -> none  [the longest x27 33.2 us: offset_step(): products = jnp.dot(gathered, weight, preferred_element_type=jnp.float32)]
    pallas_call x0 -> x5, Pallas kernels: none -> 38.1 us  [the longest x1 18.3 us: per_device(): pl.pallas_call(rules_kernel, out_shape=(jax.ShapeDtypeStruct((offsets, VO...]
    all_to_all x2 -> x1, starting transfers between devices: 25.5 us -> 18.8 us  [per_device(): lax.all_to_all(send.reshape(bricks, per // 2, 2, width), 'brick', split_a...]
    unnamed x15 -> x17, local copies, waits for them, and re-layouts: 0.04 us -> 5.98 us
    ppermute x2, waiting for transfers between devices: 3.62 us -> 0.01 us  [passed_along(): return lax.ppermute(block, axis, route)]
    ppermute x2, starting transfers between devices: 5.84 us -> 7.95 us  [passed_along(): return lax.ppermute(block, axis, route)]
  transfers between devices with their start and end apart: 4 -> 3, of which waited for: 3 -> 1; matrix products, arithmetic and copies ran while one was open for 3% -> 2% of each run, Pallas kernels for 0% -> 36%
where the time goes in v1:
time: 83.5 us; the launch traced here: 82.9 us
  Pallas kernels  38.1 us (46%)
  starting transfers between devices  26.7 us (32%)
  waiting for transfers between devices  11.3 us (14%)
  local copies, waits for them, and re-layouts  6.74 us (8%)
    all_to_all x1, starting transfers between devices, per_device(): lax.all_to_all(send.reshape(bricks, per // 2, 2, width), 'brick', split_a...  18.8 us
    pallas_call x1, Pallas kernels, per_device(): pl.pallas_call(rules_kernel, out_shape=(jax.ShapeDtypeStruct((offsets, VO...  18.3 us
    all_to_all x1, waiting for transfers between devices, per_device(): lax.all_to_all(send.reshape(bricks, per // 2, 2, width), 'brick', split_a...  11.2 us
    pallas_call x1, Pallas kernels, per_device(): pl.pallas_call(own_kernel, out_shape=jax.ShapeDtypeStruct((VOX, width), F...  11.2 us
    ppermute x2, starting transfers between devices, passed_along(): return lax.ppermute(block, axis, route)  7.95 us
    unnamed x17, local copies, waits for them, and re-layouts  5.98 us
    pallas_call x1, Pallas kernels, per_device(): pl.pallas_call(functools.partial(voxel_kernel, bricks, cap), out_shape=(j...  4.59 us
    pallas_call x1, Pallas kernels, per_device(): pl.pallas_call(functools.partial(prep_kernel, bricks, cap), out_shape=jax...  2.96 us
  transfers between devices with their start and end apart: 3, of which 1 were waited for; matrix products, arithmetic and copies ran while one was open for 2% of the time, Pallas kernels for 36%

profile of v1, /device:TPU:6, one launch (start us, length us, event | category | flops | bytes accessed | tf_op | source)
XLA Modules:
  0.0 82.9 jit_solution(16223215936023484563)
XLA Ops:
  0.0 0.0 copy-start.4
  0.0 1.1 %copy-done.4 = bf16[1024,384]{1,0:T(8,128)(2,1)S(1)} copy-done((bf16[1024,384]{1,0:T(8,128)(2,1)S(1)}, bf16[1024,384]{1,0:T(8,128)(2,1)}, u32[]{:S(2)}) %copy-start.4) | copy-done | bytes 786456
  1.1 0.0 copy-start.5
  1.1 0.9 %copy-done.5 = bf16[384,128]{1,0:T(8,128)(2,1)S(1)} copy-done((bf16[384,128]{1,0:T(8,128)(2,1)S(1)}, bf16[384,128]{1,0:T(8,128)(2,1)}, u32[]{:S(2)}) %copy-start.5) | copy-done | bytes 98328
  2.0 0.0 copy-start.6
  2.0 0.7 copy-done.6
  2.7 0.0 copy-start.7
  2.7 0.7 copy-done.7
  3.4 3.0 %prep.1 = bf16[2176,128]{1,0:T(8,128)(2,1)} custom-call(s32[1]{0:T(128)} %bitcast.1.me_ref, s32[8,128]{1,0:T(8,128)S(1)} %bitcast.17, bf16[1024,384]{1,0:T(8,128)(2,1)S(1)} %copy-done.4, bf16[384,128]{1,0:T(8,128)(2,1)S(1)} %copy-done.5, s32[1,128]{1,0:T(1,128)S(1)} %copy-done.7), custom_call_target="tpu_custom_call" | custom-call | flops 641728512 | bytes 2000000 | tf_op jit(solution)/shard_map/prep/pallas_call | solution.py:205
  6.3 18.8 %all-to-all-start = ((bf16[64,17,2,128]{3,2,1,0:T(2,128)(2,1)}), bf16[64,17,2,128]{3,2,1,0:T(2,128)(2,1)S(1)}, u32[]{:S(2)}, u32[]{:S(2)}) async-start(bf16[64,17,2,128]{3,2,1,0:T(2,128)(2,1)} %bitcast.3), calls=%async_computation | async-start | bytes 1114112 | tf_op jit(solution)/shard_map/all_to_all | solution.py:215
  25.1 0.8 reshape.34.halo_ref
  25.9 0.9 %copy_bitcast_fusion = (s32[27,512]{1,0:T(8,128)S(1)}, s32[27,512]{1,0:T(8,128)S(1)}) fusion(s32[1,27,512]{2,0,1:T(1,128)} %param.16, s32[1,27,512]{2,0,1:T(1,128)} %param.15), kind=kLoop, calls=%fused_computation | loop fusion | bytes 221184
  26.8 0.0 copy-start.1
  26.8 0.0 copy-start.2
  26.8 18.3 %rules.1 = (bf16[27,512,512]{2,1,0:T(8,128)(2,1)}, bf16[27,128,512]{2,1,0:T(8,128)(2,1)S(1)}) custom-call(s32[27,512]{1,0:T(8,128)S(1)} %get-tuple-element.16.rule_in_ref, s32[27,512]{1,0:T(8,128)S(1)} %get-tuple-element.15.rule_out_ref), custom_call_target="tpu_custom_call" | custom-call | flops 9059696640 | bytes 17694720 | tf_op jit(solution)/shard_map/rules/pallas_call | solution.py:219
  45.1 0.0 copy-start
  45.1 1.7 %copy-done = bf16[27,128,512]{2,1,0:T(8,128)(2,1)} copy-done((bf16[27,128,512]{2,1,0:T(8,128)(2,1)}, bf16[27,128,512]{2,1,0:T(8,128)(2,1)S(1)}, u32[]{:S(2)}) %copy-start) | copy-done | bytes 3538968
  46.9 0.0 copy-start.3
  46.9 11.2 %all-to-all-done = bf16[64,17,2,128]{3,2,1,0:T(2,128)(2,1)S(1)} async-done(((bf16[64,17,2,128]{3,2,1,0:T(2,128)(2,1)}), bf16[64,17,2,128]{3,2,1,0:T(2,128)(2,1)S(1)}, u32[]{:S(2)}, u32[]{:S(2)}) %all-to-all-start) | async-done | bytes 557088 | tf_op jit(solution)/shard_map/all_to_all | solution.py:215
  58.1 0.0 copy-done.1
  58.1 0.0 copy-done.2
  58.1 4.6 %voxel.1 = (bf16[512,128]{1,0:T(8,128)(2,1)S(1)}, bf16[64,128]{1,0:T(8,128)(2,1)S(1)}, bf16[64,128]{1,0:T(8,128)(2,1)S(1)}) custom-call(bf16[2176,128]{1,0:T(8,128)(2,1)S(1)} %bitcast.15, s32[17,128]{1,0:T(8,128)S(1)} %copy-done.2, bf16[3456,512]{1,0:T(8,128)(2,1)} %bitcast.12, bf16[3456,128]{1,0:T(8,128)(2,1)S(1)} %bitcast.13), custom_call_target="tpu_custom_call" | custom-call | flops 452984832 | bytes 6000000 | tf_op jit(solution)/shard_map/voxel/pallas_call | solution.py:236
  62.7 2.9 %collective-permute-start = (bf16[64,128]{1,0:T(8,128)(2,1)S(1)}, bf16[64,128]{1,0:T(8,128)(2,1)S(1)}, u32[]{:S(2)}, u32[]{:S(2)}) collective-permute-start(bf16[64,128]{1,0:T(8,128)(2,1)S(1)} %get-tuple-element.13), channel_id=1, source_target_pairs={{0,1},{1,2},{2,3},{3,4},{4,5},{5,6},{6,7},{7,8},{8,9},{9,10},{10,1... | collective-permute-start | bytes 49160 | tf_op jit(solution)/shard_map/ppermute | solution.py:21
  65.6 5.1 %collective-permute-start.1 = (bf16[64,128]{1,0:T(8,128)(2,1)S(1)}, bf16[64,128]{1,0:T(8,128)(2,1)S(1)}, u32[]{:S(2)}, u32[]{:S(2)}) collective-permute-start(bf16[64,128]{1,0:T(8,128)(2,1)S(1)} %get-tuple-element.14), channel_id=1, source_target_pairs={{1,0},{2,1},{3,2},{4,3},{5,4},{6,5},{7,6},{8,7},{9,8},{10,9},{11,1... | collective-permute-start | bytes 49160 | tf_op jit(solution)/shard_map/ppermute | solution.py:21
  70.7 11.2 %own.1.own_ref = f32[512,128]{1,0:T(8,128)S(1)} custom-call(bf16[13824,512]{1,0:T(8,128)(2,1)} %bitcast.18, bf16[512,128]{1,0:T(8,128)(2,1)S(1)} %get-tuple-element.12.voxels_ref, bf16[3456,128]{1,0:T(8,128)(2,1)S(1)} %bitcast.14), custom_call_target="tpu_custom_call" | custom-call | flops 2264924160 | bytes 14155776 | tf_op jit(solution)/shard_map/own/pallas_call | solution.py:254
  81.9 0.0 collective-permute-done.from_lower_ref
  82.0 0.0 collective-permute-done.1.from_upper_ref
  82.0 0.0 copy-done.3
  82.0 1.0 %final.1 = bf16[512,128]{1,0:T(8,128)(2,1)} custom-call(f32[512,128]{1,0:T(8,128)S(1)} %own.1.own_ref, bf16[512,128]{1,0:T(8,128)(2,1)S(1)} %get-tuple-element.12.voxels_ref, s32[1,128]{1,0:T(1,128)S(1)} %reshape.34.halo_ref, bf16[64,128]{1,0:T(8,128)(2,1)S(1)} %collective-permute-done.from_lower_ref, ...), custom_call_target="tpu_custom_call" | custom-call | flops 16777216 | bytes 1000000 | tf_op jit(solution)/shard_map/final/pallas_call | solution.py:269
Async XLA Ops:
  0.0 1.1 %copy-start.4 = (bf16[1024,384]{1,0:T(8,128)(2,1)S(1)}, bf16[1024,384]{1,0:T(8,128)(2,1)}, u32[]{:S(2)}) copy-start(bf16[1024,384]{1,0:T(8,128)(2,1)} %tokens_ref.1) | copy-start | bytes 2359300
  1.1 0.9 %copy-start.5 = (bf16[384,128]{1,0:T(8,128)(2,1)S(1)}, bf16[384,128]{1,0:T(8,128)(2,1)}, u32[]{:S(2)}) copy-start(bf16[384,128]{1,0:T(8,128)(2,1)} %weight_ref.1) | copy-start | bytes 294916
  2.0 0.7 copy-start.6
  2.7 0.7 copy-start.7
  6.3 51.8 %all-to-all-start = ((bf16[64,17,2,128]{3,2,1,0:T(2,128)(2,1)}), bf16[64,17,2,128]{3,2,1,0:T(2,128)(2,1)S(1)}, u32[]{:S(2)}, u32[]{:S(2)}) async-start(bf16[64,17,2,128]{3,2,1,0:T(2,128)(2,1)} %bitcast.3), calls=%async_computation | async-start | bytes 1114112 | tf_op jit(solution)/shard_map/all_to_all | solution.py:215
  26.8 31.4 %copy-start.1 = (bf16[27,128,128]{2,1,0:T(8,128)(2,1)S(1)}, bf16[27,128,128]{2,1,0:T(8,128)(2,1)}, u32[]{:S(2)}) copy-start(bf16[27,128,128]{2,1,0:T(8,128)(2,1)} %param.13) | copy-start | bytes 2654212
  26.8 31.4 %copy-start.2 = (s32[17,128]{1,0:T(8,128)S(1)}, s32[17,128]{1,0:T(8,128)}, u32[]{:S(2)}) copy-start(s32[17,128]{1,0:T(8,128)} %constant.8.clone.class_ref) | copy-start | bytes 26116
  45.1 1.7 %copy-start = (bf16[27,128,512]{2,1,0:T(8,128)(2,1)}, bf16[27,128,512]{2,1,0:T(8,128)(2,1)S(1)}, u32[]{:S(2)}) copy-start(bf16[27,128,512]{2,1,0:T(8,128)(2,1)S(1)} %get-tuple-element.11) | copy-start | bytes 10616836
  46.9 35.1 %copy-start.3 = (f32[128]{0:T(128)S(1)}, f32[128]{0:T(128)}, u32[]{:S(2)}) copy-start(f32[128]{0:T(128)} %param.14) | copy-start | bytes 1540
  62.7 19.2 %collective-permute-start = (bf16[64,128]{1,0:T(8,128)(2,1)S(1)}, bf16[64,128]{1,0:T(8,128)(2,1)S(1)}, u32[]{:S(2)}, u32[]{:S(2)}) collective-permute-start(bf16[64,128]{1,0:T(8,128)(2,1)S(1)} %get-tuple-element.13), channel_id=1, source_target_pairs={{0,1},{1,2},{2,3},{3,4},{4,5},{5,6},{6,7},{7,8},{8,9},{9,10},{10,1... | collective-permute-start | bytes 49160 | tf_op jit(solution)/shard_map/ppermute | solution.py:21
  65.6 16.4 %collective-permute-start.1 = (bf16[64,128]{1,0:T(8,128)(2,1)S(1)}, bf16[64,128]{1,0:T(8,128)(2,1)S(1)}, u32[]{:S(2)}, u32[]{:S(2)}) collective-permute-start(bf16[64,128]{1,0:T(8,128)(2,1)S(1)} %get-tuple-element.14), channel_id=1, source_target_pairs={{1,0},{2,1},{3,2},{4,3},{5,4},{6,5},{7,6},{8,7},{9,8},{10,9},{11,1... | collective-permute-start | bytes 49160 | tf_op jit(solution)/shard_map/ppermute | solution.py:21

commit v2 on v1

--- a/solution.py
+++ b/solution.py
@@ -12,13 +12,13 @@
 LANES = 128
 BF = jnp.bfloat16
 F32 = jnp.float32
-VMEM_LIMIT = 50 * 1024 * 1024
-
-
-def passed_along(block, axis, distance):
-    devices = range(lax.axis_size(axis))
-    route = [(i - distance, i) for i in devices if i - distance in devices]
-    return lax.ppermute(block, axis, route)
+PREP_MIB, RULES_MIB, VOXEL_MIB, OWN_MIB, FINAL_MIB = 16, 8, 16, 20, 4
+NEAR, FAR_PARTS, PACK = 12, 5, 256
+
+
+def exchanged(block, axis, first):
+    pairs = [(i, i + 1) for i in range(first, lax.axis_size(axis) - 1, 2)]
+    return lax.ppermute(block, axis, pairs + [(b, a) for a, b in pairs])
 
 
 def dot(a, b):
@@ -41,11 +41,21 @@
     )
 
 
-def prep_kernel(bricks, cap, me_ref, voxel_ref, tokens_ref, weight_ref, extra_ref, out_ref):
+def prep_kernel(
+    bricks, cap, me_ref, voxel_hbm, tokens_hbm, weight_hbm, out_hbm, voxel_ref, tokens_ref, weight_ref, out_ref, sems, out_sems
+):
+    copies = [
+        pltpu.make_async_copy(src, dst, sems.at[i])
+        for i, (src, dst) in enumerate(
+            [(voxel_hbm, voxel_ref), (weight_hbm, weight_ref), (tokens_hbm, tokens_ref)]
+        )
+    ]
+    for copy in copies:
+        copy.start()
+    copies[0].wait()
     per = cap + 2
     rows = bricks * per
     chunks = voxel_ref.shape[0]
-    projected = dot(tokens_ref[...], weight_ref[...]).astype(BF)
     t_from = lax.broadcasted_iota(jnp.int32, (LANES, LANES), 0)
     t_to = lax.broadcasted_iota(jnp.int32, (LANES, LANES), 1)
     upper = jnp.where(t_from <= t_to, 1.0, 0.0).astype(BF)
@@ -71,14 +81,23 @@
     slot_rows = dot_t(
         jnp.concatenate(member, axis=1).astype(BF), jnp.concatenate(slot_cols, axis=1)
     ).astype(BF)
+    column = lax.broadcasted_iota(jnp.int32, (1, LANES), 1)
+    position.append(jnp.where(column < bricks, column * per + cap, (column - bricks) * per + cap + 1))
+    copies[1].wait()
+    copies[2].wait()
+    projected = dot(tokens_ref[...], weight_ref[...]).astype(BF)
     source = jnp.concatenate([projected, slot_rows[:, :LANES], slot_rows[:, LANES:]], axis=0)
-    position.append(extra_ref[...])
-    size = 256
-    for start in range(0, rows, size):
-        n = min(size, rows - start)
+    sends = []
+    for i, start in enumerate(range(0, rows, PACK)):
+        n = min(PACK, rows - start)
         numbers = row_iota(n)
         table = jnp.concatenate([one_hot_rows(numbers, p, start) for p in position], axis=1)
         out_ref[start : start + n, :] = dot(table, source).astype(BF)
+        part = pl.ds(start, n)
+        sends.append(pltpu.make_async_copy(out_ref.at[part], out_hbm.at[part], out_sems.at[i]))
+        sends[i].start()
+    for send in sends:
+        send.wait()
 
 
 def rules_kernel(rule_in_ref, rule_out_ref, own_ref, edge_ref):
@@ -98,8 +117,8 @@
         )
 
     pick = jnp.concatenate([table(source, s, 256) for s in range(0, VOX, 256)], axis=0)
-    for s in range(0, VOX, 256):
-        own_ref[0, s : s + 256, :] = dot_t(table(target, s, 256), pick).astype(BF)
+    place = jnp.concatenate([table(target, s, 256) for s in range(0, VOX, 256)], axis=0)
+    own_ref[0] = dot_t(pick, place).astype(BF)
     edge_ref[0] = dot_t(table(target, VOX, edge_ref.shape[1]), pick).astype(BF)
 
 
@@ -112,7 +131,19 @@
     return dot(side, weights)
 
 
-def voxel_kernel(bricks, cap, arrived_ref, class_ref, edge_counts_ref, conv_ref, voxels_ref, lower_ref, upper_ref):
+def voxel_kernel(
+    bricks, cap, me_ref, arrived_ref, class_ref, edge_hbm, conv_hbm, own_hbm,
+    voxels_ref, first_ref, second_ref, conv_ref, near_ref, edge_counts_ref, sems,
+):
+    near = near_ref.shape[0]
+    copies = [
+        pltpu.make_async_copy(src, dst, sems.at[i])
+        for i, (src, dst) in enumerate(
+            [(edge_hbm, edge_counts_ref), (conv_hbm, conv_ref), (own_hbm.at[pl.ds(0, near)], near_ref)]
+        )
+    ]
+    for copy in copies:
+        copy.start()
     per = cap + 2
     chunks = class_ref.shape[0]
     arrived = arrived_ref[...]
@@ -148,23 +179,49 @@
         parts.append((both[:, :LANES] / jnp.maximum(both[:, LANES:], 1.0)).astype(BF))
     voxels = jnp.concatenate(parts, axis=0)
     voxels_ref[...] = voxels
+    copies[0].wait()
+    copies[1].wait()
     edge = mix(edge_counts_ref[...], voxels, conv_ref[...]).astype(BF)
-    half = lower_ref.shape[0]
-    lower_ref[...] = edge[:half]
-    upper_ref[...] = edge[half:]
-
-
-def own_kernel(counts_ref, voxels_ref, conv_ref, out_ref):
-    @pl.when(pl.program_id(0) == 0)
-    def _():
-        out_ref[...] = jnp.zeros_like(out_ref)
-
-    out_ref[...] += mix(counts_ref[...], voxels_ref[...], conv_ref[...])
-
-
-def final_kernel(own_ref, voxels_ref, halo_ref, from_lower_ref, from_upper_ref, gain_ref, out_ref):
+    half = first_ref.shape[0]
+    odd = me_ref[0] % 2 == 1
+    first_ref[...] = jnp.where(odd, edge[:half], edge[half:])
+    second_ref[...] = jnp.where(odd, edge[half:], edge[:half])
+    copies[2].wait()
+
+
+def own_kernel(near_ref, own_hbm, voxels_ref, conv_ref, out_ref, far_ref, sems):
+    near, far = near_ref.shape[0], far_ref.shape[0]
+    parts = sems.shape[0]
+    size = far // parts
+    copies = [
+        pltpu.make_async_copy(
+            own_hbm.at[pl.ds(near + c * size, size)], far_ref.at[pl.ds(c * size, size)], sems.at[c]
+        )
+        for c in range(parts)
+    ]
+    for copy in copies:
+        copy.start()
+    width = voxels_ref.shape[1]
+    starts = range(0, conv_ref.shape[0], width)
+    wide = jnp.concatenate([conv_ref[s : s + width, :] for s in starts], axis=1)
+    terms = lax.dot_general(
+        wide, voxels_ref[...], (((0,), (1,)), ((), ())), preferred_element_type=F32
+    ).astype(BF)
+    side = jnp.concatenate([terms[s : s + width] for s in starts], axis=1)
+    total = dot(side[:, :near], near_ref[...])
+    for c in range(parts):
+        copies[c].wait()
+        begin = c * size
+        total += dot(side[:, near + begin : near + begin + size], far_ref[begin : begin + size, :])
+    out_ref[...] = total.T
+
+
+def final_kernel(me_ref, own_ref, voxels_ref, halo_ref, first_ref, second_ref, gain_ref, out_ref):
     numbers = row_iota(256)
-    partial = jnp.concatenate([from_lower_ref[...], from_upper_ref[...]], axis=0)
+    odd = me_ref[0] % 2 == 1
+    first, second = first_ref[...], second_ref[...]
+    lower, upper = jnp.where(odd, first, second), jnp.where(odd, second, first)
+    partial = jnp.concatenate([lower, upper], axis=0)
     for s in range(0, VOX, 256):
         place = one_hot_rows(numbers, halo_ref[...], s)
         conv_sum = own_ref[s : s + 256, :] + dot(place, partial)
@@ -173,8 +230,12 @@
         out_ref[s : s + 256, :] = (voxels_ref[s : s + 256, :].astype(F32) + fresh).astype(BF)
 
 
-def params(semantics=None):
-    return pltpu.CompilerParams(vmem_limit_bytes=VMEM_LIMIT, dimension_semantics=semantics)
+def params(mib, semantics=None):
+    return pltpu.CompilerParams(vmem_limit_bytes=mib * 1024 * 1024, dimension_semantics=semantics)
+
+
+def in_hbm(x):
+    return pltpu.with_memory_space_constraint(x, pltpu.HBM)
 
 
 def cost(flops, moved):
@@ -197,20 +258,28 @@
     brick_of, rank_of = row_number // per, row_number % per
     classes = np.where(rank_of >= cap, (rank_of - cap) * bricks + brick_of, -1)
     classes = jnp.asarray(classes.reshape(rows // LANES, LANES), jnp.int32)
-    extra = np.concatenate([np.arange(bricks) * per + cap, np.arange(bricks) * per + cap + 1])
-    extra = jnp.asarray(extra.reshape(1, 2 * bricks), jnp.int32)
     conv_rows = conv_weight.reshape(offsets * width, width)
     vmem = pl.BlockSpec(memory_space=pltpu.VMEM)
+    hbm = pl.BlockSpec(memory_space=pl.ANY)
+    smem = pl.BlockSpec(memory_space=pltpu.SMEM)
 
     send = pl.pallas_call(
         functools.partial(prep_kernel, bricks, cap),
-        out_shape=jax.ShapeDtypeStruct((rows, width), BF),
-        in_specs=[pl.BlockSpec(memory_space=pltpu.SMEM)] + [vmem] * 4,
-        out_specs=vmem,
-        compiler_params=params(),
+        out_shape=pltpu.HBM((rows, width), BF),
+        in_specs=[smem] + [hbm] * 3,
+        out_specs=hbm,
+        scratch_shapes=[
+            pltpu.VMEM((tok_count // LANES, LANES), jnp.int32),
+            pltpu.VMEM(tokens.shape, BF),
+            pltpu.VMEM(in_weight.shape, BF),
+            pltpu.VMEM((rows, width), BF),
+            pltpu.SemaphoreType.DMA((3,)),
+            pltpu.SemaphoreType.DMA((-(-rows // PACK),)),
+        ],
+        compiler_params=params(PREP_MIB),
         cost_estimate=cost(2 * rows * 1152 * width, 2_000_000),
         name="prep",
-    )(me, token_voxel.reshape(tok_count // LANES, LANES), tokens, in_weight, extra)
+    )(me, *[in_hbm(x) for x in (token_voxel.reshape(tok_count // LANES, LANES), tokens, in_weight)])
 
     arrived = lax.all_to_all(
         send.reshape(bricks, per // 2, 2, width), "brick", split_axis=0, concat_axis=0, tiled=True
@@ -219,8 +288,8 @@
     own_counts, edge_counts = pl.pallas_call(
         rules_kernel,
         out_shape=(
-            jax.ShapeDtypeStruct((offsets, VOX, VOX), BF),
-            jax.ShapeDtypeStruct((offsets, edges, VOX), BF),
+            pltpu.HBM((offsets, VOX, VOX), BF),
+            pltpu.HBM((offsets, edges, VOX), BF),
         ),
         grid=(offsets,),
         in_specs=[pl.BlockSpec((offsets, pairs), lambda k: (0, 0))] * 2,
@@ -228,53 +297,54 @@
             pl.BlockSpec((1, VOX, VOX), lambda k: (k, 0, 0)),
             pl.BlockSpec((1, edges, VOX), lambda k: (k, 0, 0)),
         ),
-        compiler_params=params(("arbitrary",)),
+        compiler_params=params(RULES_MIB, ("arbitrary",)),
         cost_estimate=cost(2 * offsets * (VOX + edges) * VOX * pairs, 2 * offsets * (VOX + edges) * VOX),
         name="rules",
     )(rule_in[0], rule_out[0])
 
-    voxels, to_lower, to_upper = pl.pallas_call(
+    own_counts = in_hbm(own_counts.reshape(offsets * VOX, VOX))
+    edge_counts = in_hbm(edge_counts.reshape(offsets * edges, VOX))
+    near = NEAR * VOX
+    voxels, first, second, conv_near, near_counts = pl.pallas_call(
         functools.partial(voxel_kernel, bricks, cap),
         out_shape=(
             jax.ShapeDtypeStruct((VOX, width), BF),
             jax.ShapeDtypeStruct((edges // 2, width), BF),
             jax.ShapeDtypeStruct((edges // 2, width), BF),
+            pltpu.VMEM((offsets * width, width), BF),
+            pltpu.VMEM((near, VOX), BF),
         ),
-        in_specs=[vmem] * 4,
-        out_specs=(vmem, vmem, vmem),
-        compiler_params=params(),
+        in_specs=[smem] + [vmem] * 2 + [hbm] * 3,
+        out_specs=(vmem,) * 5,
+        scratch_shapes=[pltpu.VMEM((offsets * edges, VOX), BF), pltpu.SemaphoreType.DMA((3,))],
+        compiler_params=params(VOXEL_MIB),
         cost_estimate=cost(2 * offsets * edges * VOX * width, 6_000_000),
         name="voxel",
-    )(arrived, classes, edge_counts.reshape(offsets * edges, VOX), conv_rows)
-
-    from_lower = passed_along(to_upper, "brick", 1)
-    from_upper = passed_along(to_lower, "brick", -1)
-
-    group = 3
+    )(me, arrived, classes, edge_counts, in_hbm(conv_rows), own_counts)
+
+    from_first = exchanged(first, "brick", 0)
+    from_second = exchanged(second, "brick", 1)
+
     own = pl.pallas_call(
         own_kernel,
         out_shape=jax.ShapeDtypeStruct((VOX, width), F32),
-        grid=(offsets // group,),
-        in_specs=[
-            pl.BlockSpec((group * VOX, VOX), lambda k: (k, 0)),
-            pl.BlockSpec((VOX, width), lambda k: (0, 0)),
-            pl.BlockSpec((group * width, width), lambda k: (k, 0)),
-        ],
-        out_specs=pl.BlockSpec((VOX, width), lambda k: (0, 0)),
-        compiler_params=params(("arbitrary",)),
+        in_specs=[vmem, hbm, vmem, vmem],
+        out_specs=vmem,
+        scratch_shapes=[pltpu.VMEM((offsets * VOX - near, VOX), BF), pltpu.SemaphoreType.DMA((FAR_PARTS,))],
+        compiler_params=params(OWN_MIB),
         cost_estimate=cost(2 * offsets * VOX * (VOX + width) * width, 2 * offsets * VOX * VOX),
         name="own",
-    )(own_counts.reshape(offsets * VOX, VOX), voxels, conv_rows)
+    )(near_counts, own_counts, voxels, conv_near)
 
     return pl.pallas_call(
         final_kernel,
         out_shape=jax.ShapeDtypeStruct((VOX, width), BF),
-        in_specs=[vmem] * 6,
+        in_specs=[smem] + [vmem] * 6,
         out_specs=vmem,
-        compiler_params=params(),
+        compiler_params=params(FINAL_MIB),
         cost_estimate=cost(2 * VOX * width * width, 1_000_000),
         name="final",
-    )(own, voxels, halo_slots.reshape(1, edges), from_lower, from_upper, channel_gain.reshape(1, width))
+    )(me, own, voxels, halo_slots.reshape(1, edges), from_first, from_second, channel_gain.reshape(1, width))
 
 
 def solution(mesh):

time: 83.5 us -> 72.6 us (0.87)
  Pallas kernels: 38.1 us -> 32.7 us
  local copies, waits for them, and re-layouts: 6.74 us -> 1.63 us
  starting transfers between devices: 26.7 us -> 25.1 us
  waiting for transfers between devices: 11.3 us -> 12.8 us
    pallas_call x1, Pallas kernels: 11.2 us -> 3.84 us  [per_device(): pl.pallas_call(own_kernel, out_shape=jax.ShapeDtypeStruct((VOX, width), F...]
    unnamed x17 -> x5, local copies, waits for them, and re-layouts: 5.98 us -> 0.86 us
    ppermute x2, starting transfers between devices: 7.95 us -> 6.29 us  [exchanged(): return lax.ppermute(block, axis, pairs + [(b, a) for a, b in pairs])]
    pallas_call x2, Pallas kernels: 21.3 us -> 22.8 us  [the longest x1 19 us: per_device(): pl.pallas_call(rules_kernel, out_shape=(pltpu.HBM((offsets, VOX, VOX), BF...]
    all_to_all x1, waiting for transfers between devices: 11.2 us -> 12.3 us  [per_device(): lax.all_to_all(send.reshape(bricks, per // 2, 2, width), 'brick', split_a...]
  transfers between devices with their start and end apart: 3 -> 3, of which waited for: 1 -> 2; matrix products, arithmetic and copies ran while one was open for 2% -> 2% of each run, Pallas kernels for 36% -> 32%
where the time goes in v2:
time: 72.6 us; the launch traced here: 72.3 us
  Pallas kernels  32.7 us (45%)
  starting transfers between devices  25.1 us (35%)
  waiting for transfers between devices  12.8 us (18%)
  local copies, waits for them, and re-layouts  1.63 us (2%)
    pallas_call x1, Pallas kernels, per_device(): pl.pallas_call(rules_kernel, out_shape=(pltpu.HBM((offsets, VOX, VOX), BF...  19 us
    all_to_all x1, starting transfers between devices, per_device(): lax.all_to_all(send.reshape(bricks, per // 2, 2, width), 'brick', split_a...  18.8 us
    all_to_all x1, waiting for transfers between devices, per_device(): lax.all_to_all(send.reshape(bricks, per // 2, 2, width), 'brick', split_a...  12.3 us
    ppermute x2, starting transfers between devices, exchanged(): return lax.ppermute(block, axis, pairs + [(b, a) for a, b in pairs])  6.29 us
    pallas_call x1, Pallas kernels, per_device(): pl.pallas_call(functools.partial(voxel_kernel, bricks, cap), out_shape=(j...  5.08 us
    pallas_call x1, Pallas kernels, per_device(): pl.pallas_call(own_kernel, out_shape=jax.ShapeDtypeStruct((VOX, width), F...  3.84 us
    pallas_call x1, Pallas kernels, per_device(): pl.pallas_call(functools.partial(prep_kernel, bricks, cap), out_shape=plt...  3.82 us
  transfers between devices with their start and end apart: 3, of which 2 were waited for; matrix products, arithmetic and copies ran while one was open for 2% of the time, Pallas kernels for 32%

profile of v2, /device:TPU:6, one launch (start us, length us, event | category | flops | bytes accessed | tf_op | source)
XLA Modules:
  0.0 72.3 jit_solution(17006563547093713226)
XLA Ops:
  0.0 3.8 %prep.1 = bf16[2176,128]{1,0:T(8,128)(2,1)} custom-call(s32[1]{0:T(128)} %bitcast.me_ref, s32[8,128]{1,0:T(8,128)} %bitcast.19, bf16[1024,384]{1,0:T(8,128)(2,1)} %tokens_hbm.1, bf16[384,128]{1,0:T(8,128)(2,1)} %weight_hbm.1), custom_call_target="tpu_custom_call" | custom-call | flops 641728512 | bytes 2000000 | tf_op jit(solution)/shard_map/prep/pallas_call | solution.py:266
  3.8 18.8 %all-to-all-start = ((bf16[64,17,2,128]{3,2,1,0:T(2,128)(2,1)}), bf16[64,17,2,128]{3,2,1,0:T(2,128)(2,1)S(1)}, u32[]{:S(2)}, u32[]{:S(2)}) async-start(bf16[64,17,2,128]{3,2,1,0:T(2,128)(2,1)} %bitcast.18), calls=%async_computation | async-start | bytes 1114112 | tf_op jit(solution)/shard_map/all_to_all | solution.py:284
  22.6 0.8 %reshape.34.halo_ref = s32[1,128]{1,0:T(1,128)S(1)} reshape(s32[1,2,64]{2,1,0:T(2,128)} %param.16) | data formatting | bytes 1024 | tf_op jit(solution)/shard_map/reshape | solution.py:347
  23.4 0.9 %copy_bitcast_fusion = (s32[27,512]{1,0:T(8,128)S(1)}, s32[27,512]{1,0:T(8,128)S(1)}) fusion(s32[1,27,512]{2,0,1:T(1,128)} %param.15, s32[1,27,512]{2,0,1:T(1,128)} %param.14), kind=kLoop, calls=%fused_computation | loop fusion | bytes 221184
  24.3 0.0 copy-start
  24.3 19.0 %rules.1 = (bf16[27,512,512]{2,1,0:T(8,128)(2,1)}, bf16[27,128,512]{2,1,0:T(8,128)(2,1)}) custom-call(s32[27,512]{1,0:T(8,128)S(1)} %get-tuple-element.20.rule_in_ref, s32[27,512]{1,0:T(8,128)S(1)} %get-tuple-element.19.rule_out_ref), custom_call_target="tpu_custom_call" | custom-call | flops 9059696640 | bytes 17694720 | tf_op jit(solution)/shard_map/rules/pallas_call | solution.py:288
  43.3 12.3 %all-to-all-done = bf16[64,17,2,128]{3,2,1,0:T(2,128)(2,1)S(1)} async-done(((bf16[64,17,2,128]{3,2,1,0:T(2,128)(2,1)}), bf16[64,17,2,128]{3,2,1,0:T(2,128)(2,1)S(1)}, u32[]{:S(2)}, u32[]{:S(2)}) %all-to-all-start) | async-done | bytes 557088 | tf_op jit(solution)/shard_map/all_to_all | solution.py:284
  55.6 0.0 copy-done
  55.6 5.1 %voxel.1 = (bf16[512,128]{1,0:T(8,128)(2,1)S(1)}, bf16[64,128]{1,0:T(8,128)(2,1)S(1)}, bf16[64,128]{1,0:T(8,128)(2,1)S(1)}, bf16[3456,128]{1,0:T(8,128)(2,1)S(1)}, bf16[6144,512]{1,0:T(8,128)(2,1)S(1)}) custom-call(s32[1]{0:T(128)} %bitcast.me_ref, bf16[2176,128]{1,0:T(8,128)(2,1)S(1)} %bitcast.12, s32[17,128]{1,0:T(8,128)S(1)} %copy-done, ...), custom_call_target="tpu_custom_call" | custom-call | flops 452984832 | bytes 6000000 | tf_op jit(solution)/shard_map/voxel/pallas_call | solution.py:308
  60.7 2.9 %collective-permute-start = (bf16[64,128]{1,0:T(8,128)(2,1)S(1)}, bf16[64,128]{1,0:T(8,128)(2,1)S(1)}, u32[]{:S(2)}, u32[]{:S(2)}) collective-permute-start(bf16[64,128]{1,0:T(8,128)(2,1)S(1)} %get-tuple-element.17), channel_id=1, source_target_pairs={{0,1},{2,3},{4,5},{6,7},{8,9},{10,11},{12,13},{14,15},{16,17},{18,... | collective-permute-start | bytes 49160 | tf_op jit(solution)/shard_map/ppermute | solution.py:21
  63.6 3.4 %collective-permute-start.1 = (bf16[64,128]{1,0:T(8,128)(2,1)S(1)}, bf16[64,128]{1,0:T(8,128)(2,1)S(1)}, u32[]{:S(2)}, u32[]{:S(2)}) collective-permute-start(bf16[64,128]{1,0:T(8,128)(2,1)S(1)} %get-tuple-element.18), channel_id=1, source_target_pairs={{1,2},{3,4},{5,6},{7,8},{9,10},{11,12},{13,14},{15,16},{17,18},{19... | collective-permute-start | bytes 49160 | tf_op jit(solution)/shard_map/ppermute | solution.py:21
  67.0 0.0 copy-start.1
  67.0 3.8 %own.1.own_ref = f32[512,128]{1,0:T(8,128)S(1)} custom-call(bf16[6144,512]{1,0:T(8,128)(2,1)S(1)} %get-tuple-element.14.near_ref, bf16[13824,512]{1,0:T(8,128)(2,1)} %bitcast.15, bf16[512,128]{1,0:T(8,128)(2,1)S(1)} %get-tuple-element.15.voxels_ref, bf16[3456,128]{1,0:T(8,128)(2,1)S(1)} %get-tuple-element.16.conv_ref), custom_call_target="tpu_custom_call" | custom-call | flops 2264924160 | bytes 14155776 | tf_op jit(solution)/shard_map/own/pallas_call | solution.py:328
  70.9 0.0 collective-permute-done.first_ref
  70.9 0.4 collective-permute-done.1.second_ref
  71.3 0.0 copy-done.1
  71.3 1.0 %final.1 = bf16[512,128]{1,0:T(8,128)(2,1)} custom-call(s32[1]{0:T(128)} %bitcast.me_ref, f32[512,128]{1,0:T(8,128)S(1)} %own.1.own_ref, bf16[512,128]{1,0:T(8,128)(2,1)S(1)} %get-tuple-element.15.voxels_ref, s32[1,128]{1,0:T(1,128)S(1)} %reshape.34.halo_ref, bf16[64,128]{1,0:T(8,128)(2,1)S(1)} %collective-permute-done.first_ref, ...), custom_call_target="tpu_custom_call" | custom-call | flops 16777216 | bytes 1000000 | tf_op jit(solution)/shard_map/final/pallas_call | solution.py:339
Async XLA Ops:
  3.8 51.8 %all-to-all-start = ((bf16[64,17,2,128]{3,2,1,0:T(2,128)(2,1)}), bf16[64,17,2,128]{3,2,1,0:T(2,128)(2,1)S(1)}, u32[]{:S(2)}, u32[]{:S(2)}) async-start(bf16[64,17,2,128]{3,2,1,0:T(2,128)(2,1)} %bitcast.18), calls=%async_computation | async-start | bytes 1114112 | tf_op jit(solution)/shard_map/all_to_all | solution.py:284
  24.3 31.4 %copy-start = (s32[17,128]{1,0:T(8,128)S(1)}, s32[17,128]{1,0:T(8,128)}, u32[]{:S(2)}) copy-start(s32[17,128]{1,0:T(8,128)} %constant.6.clone.class_ref) | copy-start | bytes 26116
  60.7 10.2 %collective-permute-start = (bf16[64,128]{1,0:T(8,128)(2,1)S(1)}, bf16[64,128]{1,0:T(8,128)(2,1)S(1)}, u32[]{:S(2)}, u32[]{:S(2)}) collective-permute-start(bf16[64,128]{1,0:T(8,128)(2,1)S(1)} %get-tuple-element.17), channel_id=1, source_target_pairs={{0,1},{2,3},{4,5},{6,7},{8,9},{10,11},{12,13},{14,15},{16,17},{18,... | collective-permute-start | bytes 49160 | tf_op jit(solution)/shard_map/ppermute | solution.py:21
  63.6 7.7 %collective-permute-start.1 = (bf16[64,128]{1,0:T(8,128)(2,1)S(1)}, bf16[64,128]{1,0:T(8,128)(2,1)S(1)}, u32[]{:S(2)}, u32[]{:S(2)}) collective-permute-start(bf16[64,128]{1,0:T(8,128)(2,1)S(1)} %get-tuple-element.18), channel_id=1, source_target_pairs={{1,2},{3,4},{5,6},{7,8},{9,10},{11,12},{13,14},{15,16},{17,18},{19... | collective-permute-start | bytes 49160 | tf_op jit(solution)/shard_map/ppermute | solution.py:21
  67.0 4.3 %copy-start.1 = (f32[128]{0:T(128)S(1)}, f32[128]{0:T(128)}, u32[]{:S(2)}) copy-start(f32[128]{0:T(128)} %param.13) | copy-start | bytes 1540

commit v3 on v2

--- a/solution.py
+++ b/solution.py
@@ -13,7 +13,7 @@
 BF = jnp.bfloat16
 F32 = jnp.float32
 PREP_MIB, RULES_MIB, VOXEL_MIB, OWN_MIB, FINAL_MIB = 16, 8, 16, 20, 4
-NEAR, FAR_PARTS, PACK = 12, 5, 256
+KEEP, NEAR, FAR_PARTS, PACK = 3, 10, 4, 256
 
 
 def exchanged(block, axis, first):
@@ -100,7 +100,7 @@
         send.wait()
 
 
-def rules_kernel(rule_in_ref, rule_out_ref, own_ref, edge_ref):
+def rules_kernel(rule_in_ref, rule_out_ref, keep_ref, own_ref, edge_ref):
     k = pl.program_id(0)
     pairs = rule_in_ref.shape[1]
     source = rule_in_ref[pl.ds(k, 1), :]
@@ -118,7 +118,16 @@
 
     pick = jnp.concatenate([table(source, s, 256) for s in range(0, VOX, 256)], axis=0)
     place = jnp.concatenate([table(target, s, 256) for s in range(0, VOX, 256)], axis=0)
-    own_ref[0] = dot_t(pick, place).astype(BF)
+    counts = dot_t(pick, place).astype(BF)
+
+    @pl.when(k < KEEP)
+    def _():
+        keep_ref[0] = counts
+
+    @pl.when(k >= KEEP)
+    def _():
+        own_ref[0] = counts
+
     edge_ref[0] = dot_t(table(target, VOX, edge_ref.shape[1]), pick).astype(BF)
 
 
@@ -132,14 +141,14 @@
 
 
 def voxel_kernel(
-    bricks, cap, me_ref, arrived_ref, class_ref, edge_hbm, conv_hbm, own_hbm,
-    voxels_ref, first_ref, second_ref, conv_ref, near_ref, edge_counts_ref, sems,
+    bricks, cap, me_ref, arrived_ref, class_ref, conv_ref, edge_hbm, own_hbm,
+    voxels_ref, first_ref, second_ref, near_ref, edge_counts_ref, sems,
 ):
     near = near_ref.shape[0]
     copies = [
         pltpu.make_async_copy(src, dst, sems.at[i])
         for i, (src, dst) in enumerate(
-            [(edge_hbm, edge_counts_ref), (conv_hbm, conv_ref), (own_hbm.at[pl.ds(0, near)], near_ref)]
+            [(edge_hbm, edge_counts_ref), (own_hbm.at[pl.ds(0, near)], near_ref)]
         )
     ]
     for copy in copies:
@@ -180,17 +189,16 @@
     voxels = jnp.concatenate(parts, axis=0)
     voxels_ref[...] = voxels
     copies[0].wait()
-    copies[1].wait()
     edge = mix(edge_counts_ref[...], voxels, conv_ref[...]).astype(BF)
     half = first_ref.shape[0]
     odd = me_ref[0] % 2 == 1
     first_ref[...] = jnp.where(odd, edge[:half], edge[half:])
     second_ref[...] = jnp.where(odd, edge[half:], edge[:half])
-    copies[2].wait()
-
-
-def own_kernel(near_ref, own_hbm, voxels_ref, conv_ref, out_ref, far_ref, sems):
-    near, far = near_ref.shape[0], far_ref.shape[0]
+    copies[1].wait()
+
+
+def own_kernel(keep_ref, near_ref, own_hbm, voxels_ref, conv_ref, out_ref, far_ref, sems):
+    keep, near, far = keep_ref.shape[0], near_ref.shape[0], far_ref.shape[0]
     parts = sems.shape[0]
     size = far // parts
     copies = [
@@ -208,11 +216,12 @@
         wide, voxels_ref[...], (((0,), (1,)), ((), ())), preferred_element_type=F32
     ).astype(BF)
     side = jnp.concatenate([terms[s : s + width] for s in starts], axis=1)
-    total = dot(side[:, :near], near_ref[...])
+    total = dot(side[:, :keep], keep_ref[...]) + dot(side[:, keep : keep + near], near_ref[...])
     for c in range(parts):
         copies[c].wait()
         begin = c * size
-        total += dot(side[:, near + begin : near + begin + size], far_ref[begin : begin + size, :])
+        at = keep + near + begin
+        total += dot(side[:, at : at + size], far_ref[begin : begin + size, :])
     out_ref[...] = total.T
 
 
@@ -236,6 +245,10 @@
 
 def in_hbm(x):
     return pltpu.with_memory_space_constraint(x, pltpu.HBM)
+
+
+def in_vmem(x):
+    return pltpu.with_memory_space_constraint(x, pltpu.VMEM)
 
 
 def cost(flops, moved):
@@ -285,16 +298,18 @@
         send.reshape(bricks, per // 2, 2, width), "brick", split_axis=0, concat_axis=0, tiled=True
     ).reshape(rows, width)
 
-    own_counts, edge_counts = pl.pallas_call(
+    keep_counts, own_counts, edge_counts = pl.pallas_call(
         rules_kernel,
         out_shape=(
-            pltpu.HBM((offsets, VOX, VOX), BF),
+            pltpu.VMEM((KEEP, VOX, VOX), BF),
+            pltpu.HBM((offsets - KEEP, VOX, VOX), BF),
             pltpu.HBM((offsets, edges, VOX), BF),
         ),
         grid=(offsets,),
         in_specs=[pl.BlockSpec((offsets, pairs), lambda k: (0, 0))] * 2,
         out_specs=(
-            pl.BlockSpec((1, VOX, VOX), lambda k: (k, 0, 0)),
+            pl.BlockSpec((1, VOX, VOX), lambda k: (jnp.minimum(k, KEEP - 1), 0, 0)),
+            pl.BlockSpec((1, VOX, VOX), lambda k: (jnp.maximum(k - KEEP, 0), 0, 0)),
             pl.BlockSpec((1, edges, VOX), lambda k: (k, 0, 0)),
         ),
         compiler_params=params(RULES_MIB, ("arbitrary",)),
@@ -302,25 +317,24 @@
         name="rules",
     )(rule_in[0], rule_out[0])
 
-    own_counts = in_hbm(own_counts.reshape(offsets * VOX, VOX))
+    own_counts = in_hbm(own_counts.reshape((offsets - KEEP) * VOX, VOX))
     edge_counts = in_hbm(edge_counts.reshape(offsets * edges, VOX))
     near = NEAR * VOX
-    voxels, first, second, conv_near, near_counts = pl.pallas_call(
+    voxels, first, second, near_counts = pl.pallas_call(
         functools.partial(voxel_kernel, bricks, cap),
         out_shape=(
             jax.ShapeDtypeStruct((VOX, width), BF),
             jax.ShapeDtypeStruct((edges // 2, width), BF),
             jax.ShapeDtypeStruct((edges // 2, width), BF),
-            pltpu.VMEM((offsets * width, width), BF),
             pltpu.VMEM((near, VOX), BF),
         ),
-        in_specs=[smem] + [vmem] * 2 + [hbm] * 3,
-        out_specs=(vmem,) * 5,
-        scratch_shapes=[pltpu.VMEM((offsets * edges, VOX), BF), pltpu.SemaphoreType.DMA((3,))],
+        in_specs=[smem] + [vmem] * 3 + [hbm] * 2,
+        out_specs=(vmem,) * 4,
+        scratch_shapes=[pltpu.VMEM((offsets * edges, VOX), BF), pltpu.SemaphoreType.DMA((2,))],
         compiler_params=params(VOXEL_MIB),
         cost_estimate=cost(2 * offsets * edges * VOX * width, 6_000_000),
         name="voxel",
-    )(me, arrived, classes, edge_counts, in_hbm(conv_rows), own_counts)
+    )(me, arrived, classes, conv_rows, edge_counts, own_counts)
 
     from_first = exchanged(first, "brick", 0)
     from_second = exchanged(second, "brick", 1)
@@ -328,13 +342,13 @@
     own = pl.pallas_call(
         own_kernel,
         out_shape=jax.ShapeDtypeStruct((VOX, width), F32),
-        in_specs=[vmem, hbm, vmem, vmem],
+        in_specs=[vmem, vmem, hbm, vmem, vmem],
         out_specs=vmem,
-        scratch_shapes=[pltpu.VMEM((offsets * VOX - near, VOX), BF), pltpu.SemaphoreType.DMA((FAR_PARTS,))],
+        scratch_shapes=[pltpu.VMEM(((offsets - KEEP) * VOX - near, VOX), BF), pltpu.SemaphoreType.DMA((FAR_PARTS,))],
         compiler_params=params(OWN_MIB),
         cost_estimate=cost(2 * offsets * VOX * (VOX + width) * width, 2 * offsets * VOX * VOX),
         name="own",
-    )(near_counts, own_counts, voxels, conv_near)
+    )(in_vmem(keep_counts.reshape(KEEP * VOX, VOX)), near_counts, own_counts, voxels, conv_rows)
 
     return pl.pallas_call(
         final_kernel,

time: 72.6 us -> 72 us (level)
  waiting for transfers between devices: 12.8 us -> 8.04 us
  Pallas kernels: 32.7 us -> 36.9 us
    all_to_all x1, waiting for transfers between devices: 12.3 us -> 7.69 us  [per_device(): lax.all_to_all(send.reshape(bricks, per // 2, 2, width), 'brick', split_a...]
    pallas_call x1, Pallas kernels: 19 us -> 23.7 us  [per_device(): pl.pallas_call(rules_kernel, out_shape=(pltpu.VMEM((KEEP, VOX, VOX), BF),...]
  transfers between devices with their start and end apart: 3 -> 3, of which waited for: 2 -> 2; matrix products, arithmetic and copies ran while one was open for 2% -> 2% of each run, Pallas kernels for 32% -> 38%
where the time goes in v3:
time: 72 us; the launch traced here: 71.7 us
  Pallas kernels  36.9 us (51%)
  starting transfers between devices  25.1 us (35%)
  waiting for transfers between devices  8.04 us (11%)
  local copies, waits for them, and re-layouts  1.63 us (2%)
    pallas_call x1, Pallas kernels, per_device(): pl.pallas_call(rules_kernel, out_shape=(pltpu.VMEM((KEEP, VOX, VOX), BF),...  23.7 us
    all_to_all x1, starting transfers between devices, per_device(): lax.all_to_all(send.reshape(bricks, per // 2, 2, width), 'brick', split_a...  18.8 us
    all_to_all x1, waiting for transfers between devices, per_device(): lax.all_to_all(send.reshape(bricks, per // 2, 2, width), 'brick', split_a...  7.69 us
    ppermute x2, starting transfers between devices, exchanged(): return lax.ppermute(block, axis, pairs + [(b, a) for a, b in pairs])  6.29 us
    pallas_call x1, Pallas kernels, per_device(): pl.pallas_call(functools.partial(voxel_kernel, bricks, cap), out_shape=(j...  4.51 us
    pallas_call x1, Pallas kernels, per_device(): pl.pallas_call(own_kernel, out_shape=jax.ShapeDtypeStruct((VOX, width), F...  3.92 us
    pallas_call x1, Pallas kernels, per_device(): pl.pallas_call(functools.partial(prep_kernel, bricks, cap), out_shape=plt...  3.82 us
  transfers between devices with their start and end apart: 3, of which 2 were waited for; matrix products, arithmetic and copies ran while one was open for 2% of the time, Pallas kernels for 38%

profile of v3, /device:TPU:6, one launch (start us, length us, event | category | flops | bytes accessed | tf_op | source)
XLA Modules:
  0.0 71.7 jit_solution(7055466291406639411)
XLA Ops:
  0.0 3.8 %prep.1 = bf16[2176,128]{1,0:T(8,128)(2,1)} custom-call(s32[1]{0:T(128)} %bitcast.me_ref, s32[8,128]{1,0:T(8,128)} %bitcast.22, bf16[1024,384]{1,0:T(8,128)(2,1)} %tokens_hbm.1, bf16[384,128]{1,0:T(8,128)(2,1)} %weight_hbm.1), custom_call_target="tpu_custom_call" | custom-call | flops 641728512 | bytes 2000000 | tf_op jit(solution)/shard_map/prep/pallas_call | solution.py:279
  3.8 18.8 %all-to-all-start = ((bf16[64,17,2,128]{3,2,1,0:T(2,128)(2,1)}), bf16[64,17,2,128]{3,2,1,0:T(2,128)(2,1)S(1)}, u32[]{:S(2)}, u32[]{:S(2)}) async-start(bf16[64,17,2,128]{3,2,1,0:T(2,128)(2,1)} %bitcast.21), calls=%async_computation | async-start | bytes 1114112 | tf_op jit(solution)/shard_map/all_to_all | solution.py:297
  22.6 0.8 %reshape.38.halo_ref = s32[1,128]{1,0:T(1,128)S(1)} reshape(s32[1,2,64]{2,1,0:T(2,128)} %param.16) | data formatting | bytes 1024 | tf_op jit(solution)/shard_map/reshape | solution.py:361
  23.4 0.9 %copy_bitcast_fusion = (s32[27,512]{1,0:T(8,128)S(1)}, s32[27,512]{1,0:T(8,128)S(1)}) fusion(s32[1,27,512]{2,0,1:T(1,128)} %param.15, s32[1,27,512]{2,0,1:T(1,128)} %param.14), kind=kLoop, calls=%fused_computation | loop fusion | bytes 221184
  24.3 0.0 copy-start
  24.3 0.0 copy-start.1
  24.3 23.7 %rules.1 = (bf16[3,512,512]{2,1,0:T(8,128)(2,1)S(1)}, bf16[24,512,512]{2,1,0:T(8,128)(2,1)}, bf16[27,128,512]{2,1,0:T(8,128)(2,1)}) custom-call(s32[27,512]{1,0:T(8,128)S(1)} %get-tuple-element.20.rule_in_ref, s32[27,512]{1,0:T(8,128)S(1)} %get-tuple-element.19.rule_out_ref), custom_call_target="tpu_custom_call" | custom-call | flops 9059696640 | bytes 17694720 | tf_op jit(solution)/shard_map/rules/pallas_call | solution.py:301
  47.9 7.7 %all-to-all-done = bf16[64,17,2,128]{3,2,1,0:T(2,128)(2,1)S(1)} async-done(((bf16[64,17,2,128]{3,2,1,0:T(2,128)(2,1)}), bf16[64,17,2,128]{3,2,1,0:T(2,128)(2,1)S(1)}, u32[]{:S(2)}, u32[]{:S(2)}) %all-to-all-start) | async-done | bytes 557088 | tf_op jit(solution)/shard_map/all_to_all | solution.py:297
  55.6 0.0 copy-done
  55.6 0.0 copy-done.1
  55.6 4.5 %voxel.1 = (bf16[512,128]{1,0:T(8,128)(2,1)S(1)}, bf16[64,128]{1,0:T(8,128)(2,1)S(1)}, bf16[64,128]{1,0:T(8,128)(2,1)S(1)}, bf16[5120,512]{1,0:T(8,128)(2,1)S(1)}) custom-call(s32[1]{0:T(128)} %bitcast.me_ref, bf16[2176,128]{1,0:T(8,128)(2,1)S(1)} %bitcast.15, s32[17,128]{1,0:T(8,128)S(1)} %copy-done.1, bf16[3456,128]{1,0:T(8,128)(2,1)S(1)} %bitcast.13, ...), custom_call_target="tpu_custom_call" | custom-call | flops 452984832 | bytes 6000000 | tf_op jit(solution)/shard_map/voxel/pallas_call | solution.py:323
  60.2 2.9 %collective-permute-start = (bf16[64,128]{1,0:T(8,128)(2,1)S(1)}, bf16[64,128]{1,0:T(8,128)(2,1)S(1)}, u32[]{:S(2)}, u32[]{:S(2)}) collective-permute-start(bf16[64,128]{1,0:T(8,128)(2,1)S(1)} %get-tuple-element.17), channel_id=1, source_target_pairs={{0,1},{2,3},{4,5},{6,7},{8,9},{10,11},{12,13},{14,15},{16,17},{18,... | collective-permute-start | bytes 49160 | tf_op jit(solution)/shard_map/ppermute | solution.py:21
  63.0 3.4 %collective-permute-start.1 = (bf16[64,128]{1,0:T(8,128)(2,1)S(1)}, bf16[64,128]{1,0:T(8,128)(2,1)S(1)}, u32[]{:S(2)}, u32[]{:S(2)}) collective-permute-start(bf16[64,128]{1,0:T(8,128)(2,1)S(1)} %get-tuple-element.18), channel_id=1, source_target_pairs={{1,2},{3,4},{5,6},{7,8},{9,10},{11,12},{13,14},{15,16},{17,18},{19... | collective-permute-start | bytes 49160 | tf_op jit(solution)/shard_map/ppermute | solution.py:21
  66.5 0.0 copy-start.2
  66.5 3.9 %own.1.own_ref = f32[512,128]{1,0:T(8,128)S(1)} custom-call(bf16[1536,512]{1,0:T(8,128)(2,1)S(1)} %bitcast.16, bf16[5120,512]{1,0:T(8,128)(2,1)S(1)} %get-tuple-element.15.near_ref, bf16[12288,512]{1,0:T(8,128)(2,1)} %bitcast.19, bf16[512,128]{1,0:T(8,128)(2,1)S(1)} %get-tuple-element.16.voxels_ref, bf16[3456,128]{1,0:T(8,128)(2,1)S(1)} %bitcast.14), custom_call_target="tpu_custom_call" | custom-call | flops 2264924160 | bytes 14155776 | tf_op jit(solution)/shard_map/own/pallas_call | solution.py:342
  70.4 0.0 collective-permute-done.first_ref
  70.4 0.4 collective-permute-done.1.second_ref
  70.8 0.0 copy-done.2
  70.8 1.0 %final.1 = bf16[512,128]{1,0:T(8,128)(2,1)} custom-call(s32[1]{0:T(128)} %bitcast.me_ref, f32[512,128]{1,0:T(8,128)S(1)} %own.1.own_ref, bf16[512,128]{1,0:T(8,128)(2,1)S(1)} %get-tuple-element.16.voxels_ref, s32[1,128]{1,0:T(1,128)S(1)} %reshape.38.halo_ref, bf16[64,128]{1,0:T(8,128)(2,1)S(1)} %collective-permute-done.first_ref, ...), custom_call_target="tpu_custom_call" | custom-call | flops 16777216 | bytes 1000000 | tf_op jit(solution)/shard_map/final/pallas_call | solution.py:353
Async XLA Ops:
  3.8 51.8 %all-to-all-start = ((bf16[64,17,2,128]{3,2,1,0:T(2,128)(2,1)}), bf16[64,17,2,128]{3,2,1,0:T(2,128)(2,1)S(1)}, u32[]{:S(2)}, u32[]{:S(2)}) async-start(bf16[64,17,2,128]{3,2,1,0:T(2,128)(2,1)} %bitcast.21), calls=%async_computation | async-start | bytes 1114112 | tf_op jit(solution)/shard_map/all_to_all | solution.py:297
  24.3 31.4 %copy-start = (bf16[27,128,128]{2,1,0:T(8,128)(2,1)S(1)}, bf16[27,128,128]{2,1,0:T(8,128)(2,1)}, u32[]{:S(2)}) copy-start(bf16[27,128,128]{2,1,0:T(8,128)(2,1)} %param.12) | copy-start | bytes 2654212
  24.3 31.4 %copy-start.1 = (s32[17,128]{1,0:T(8,128)S(1)}, s32[17,128]{1,0:T(8,128)}, u32[]{:S(2)}) copy-start(s32[17,128]{1,0:T(8,128)} %constant.6.clone.class_ref) | copy-start | bytes 26116
  60.2 10.2 %collective-permute-start = (bf16[64,128]{1,0:T(8,128)(2,1)S(1)}, bf16[64,128]{1,0:T(8,128)(2,1)S(1)}, u32[]{:S(2)}, u32[]{:S(2)}) collective-permute-start(bf16[64,128]{1,0:T(8,128)(2,1)S(1)} %get-tuple-element.17), channel_id=1, source_target_pairs={{0,1},{2,3},{4,5},{6,7},{8,9},{10,11},{12,13},{14,15},{16,17},{18,... | collective-permute-start | bytes 49160 | tf_op jit(solution)/shard_map/ppermute | solution.py:21
  63.0 7.7 %collective-permute-start.1 = (bf16[64,128]{1,0:T(8,128)(2,1)S(1)}, bf16[64,128]{1,0:T(8,128)(2,1)S(1)}, u32[]{:S(2)}, u32[]{:S(2)}) collective-permute-start(bf16[64,128]{1,0:T(8,128)(2,1)S(1)} %get-tuple-element.18), channel_id=1, source_target_pairs={{1,2},{3,4},{5,6},{7,8},{9,10},{11,12},{13,14},{15,16},{17,18},{19... | collective-permute-start | bytes 49160 | tf_op jit(solution)/shard_map/ppermute | solution.py:21
  66.5 4.3 %copy-start.2 = (f32[128]{0:T(128)S(1)}, f32[128]{0:T(128)}, u32[]{:S(2)}) copy-start(f32[128]{0:T(128)} %param.13) | copy-start | bytes 1540

commit v4 on v3

--- a/solution.py
+++ b/solution.py
@@ -119,15 +119,8 @@
     pick = jnp.concatenate([table(source, s, 256) for s in range(0, VOX, 256)], axis=0)
     place = jnp.concatenate([table(target, s, 256) for s in range(0, VOX, 256)], axis=0)
     counts = dot_t(pick, place).astype(BF)
-
-    @pl.when(k < KEEP)
-    def _():
-        keep_ref[0] = counts
-
-    @pl.when(k >= KEEP)
-    def _():
-        own_ref[0] = counts
-
+    own_ref[0] = counts
+    keep_ref[0] = counts
     edge_ref[0] = dot_t(table(target, VOX, edge_ref.shape[1]), pick).astype(BF)
 
 
@@ -198,7 +191,7 @@
 
 
 def own_kernel(keep_ref, near_ref, own_hbm, voxels_ref, conv_ref, out_ref, far_ref, sems):
-    keep, near, far = keep_ref.shape[0], near_ref.shape[0], far_ref.shape[0]
+    near, far = near_ref.shape[0], far_ref.shape[0]
     parts = sems.shape[0]
     size = far // parts
     copies = [
@@ -216,11 +209,11 @@
         wide, voxels_ref[...], (((0,), (1,)), ((), ())), preferred_element_type=F32
     ).astype(BF)
     side = jnp.concatenate([terms[s : s + width] for s in starts], axis=1)
-    total = dot(side[:, :keep], keep_ref[...]) + dot(side[:, keep : keep + near], near_ref[...])
+    total = dot(side[:, near + far :], keep_ref[...]) + dot(side[:, :near], near_ref[...])
     for c in range(parts):
         copies[c].wait()
         begin = c * size
-        at = keep + near + begin
+        at = near + begin
         total += dot(side[:, at : at + size], far_ref[begin : begin + size, :])
     out_ref[...] = total.T
 
@@ -302,14 +295,14 @@
         rules_kernel,
         out_shape=(
             pltpu.VMEM((KEEP, VOX, VOX), BF),
-            pltpu.HBM((offsets - KEEP, VOX, VOX), BF),
+            pltpu.HBM((offsets - KEEP + 1, VOX, VOX), BF),
             pltpu.HBM((offsets, edges, VOX), BF),
         ),
         grid=(offsets,),
         in_specs=[pl.BlockSpec((offsets, pairs), lambda k: (0, 0))] * 2,
         out_specs=(
-            pl.BlockSpec((1, VOX, VOX), lambda k: (jnp.minimum(k, KEEP - 1), 0, 0)),
-            pl.BlockSpec((1, VOX, VOX), lambda k: (jnp.maximum(k - KEEP, 0), 0, 0)),
+            pl.BlockSpec((1, VOX, VOX), lambda k: (jnp.maximum(k - (offsets - KEEP), 0), 0, 0)),
+            pl.BlockSpec((1, VOX, VOX), lambda k: (jnp.minimum(k, offsets - KEEP), 0, 0)),
             pl.BlockSpec((1, edges, VOX), lambda k: (k, 0, 0)),
         ),
         compiler_params=params(RULES_MIB, ("arbitrary",)),
@@ -317,7 +310,7 @@
         name="rules",
     )(rule_in[0], rule_out[0])
 
-    own_counts = in_hbm(own_counts.reshape((offsets - KEEP) * VOX, VOX))
+    own_counts = in_hbm(own_counts.reshape((offsets - KEEP + 1) * VOX, VOX))
     edge_counts = in_hbm(edge_counts.reshape(offsets * edges, VOX))
     near = NEAR * VOX
     voxels, first, second, near_counts = pl.pallas_call(

time: 72 us -> 72 us (level)
  Pallas kernels: 36.9 us -> 32.1 us
  waiting for transfers between devices: 8.04 us -> 12.8 us
    all_to_all x1, waiting for transfers between devices: 7.69 us -> 12.4 us  [per_device(): lax.all_to_all(send.reshape(bricks, per // 2, 2, width), 'brick', split_a...]
    pallas_call x1, Pallas kernels: 23.7 us -> 18.9 us  [per_device(): pl.pallas_call(rules_kernel, out_shape=(pltpu.VMEM((KEEP, VOX, VOX), BF),...]
  transfers between devices with their start and end apart: 3 -> 3, of which waited for: 2 -> 2; matrix products, arithmetic and copies ran while one was open for 2% -> 2% of each run, Pallas kernels for 38% -> 32%
where the time goes in v4:
time: 72 us; the launch traced here: 71.7 us
  Pallas kernels  32.1 us (45%)
  starting transfers between devices  25.1 us (35%)
  waiting for transfers between devices  12.8 us (18%)
  local copies, waits for them, and re-layouts  1.63 us (2%)
    pallas_call x1, Pallas kernels, per_device(): pl.pallas_call(rules_kernel, out_shape=(pltpu.VMEM((KEEP, VOX, VOX), BF),...  18.9 us
    all_to_all x1, starting transfers between devices, per_device(): lax.all_to_all(send.reshape(bricks, per // 2, 2, width), 'brick', split_a...  18.8 us
    all_to_all x1, waiting for transfers between devices, per_device(): lax.all_to_all(send.reshape(bricks, per // 2, 2, width), 'brick', split_a...  12.4 us
    ppermute x2, starting transfers between devices, exchanged(): return lax.ppermute(block, axis, pairs + [(b, a) for a, b in pairs])  6.29 us
    pallas_call x1, Pallas kernels, per_device(): pl.pallas_call(functools.partial(voxel_kernel, bricks, cap), out_shape=(j...  4.5 us
    pallas_call x1, Pallas kernels, per_device(): pl.pallas_call(own_kernel, out_shape=jax.ShapeDtypeStruct((VOX, width), F...  3.93 us
    pallas_call x1, Pallas kernels, per_device(): pl.pallas_call(functools.partial(prep_kernel, bricks, cap), out_shape=plt...  3.82 us
  transfers between devices with their start and end apart: 3, of which 2 were waited for; matrix products, arithmetic and copies ran while one was open for 2% of the time, Pallas kernels for 32%

profile of v4, /device:TPU:6, one launch (start us, length us, event | category | flops | bytes accessed | tf_op | source)
XLA Modules:
  0.0 71.7 jit_solution(7898277462669106995)
XLA Ops:
  0.0 3.8 %prep.1 = bf16[2176,128]{1,0:T(8,128)(2,1)} custom-call(s32[1]{0:T(128)} %bitcast.me_ref, s32[8,128]{1,0:T(8,128)} %bitcast.22, bf16[1024,384]{1,0:T(8,128)(2,1)} %tokens_hbm.1, bf16[384,128]{1,0:T(8,128)(2,1)} %weight_hbm.1), custom_call_target="tpu_custom_call" | custom-call | flops 641728512 | bytes 2000000 | tf_op jit(solution)/shard_map/prep/pallas_call | solution.py:272
  3.8 18.8 %all-to-all-start = ((bf16[64,17,2,128]{3,2,1,0:T(2,128)(2,1)}), bf16[64,17,2,128]{3,2,1,0:T(2,128)(2,1)S(1)}, u32[]{:S(2)}, u32[]{:S(2)}) async-start(bf16[64,17,2,128]{3,2,1,0:T(2,128)(2,1)} %bitcast.21), calls=%async_computation | async-start | bytes 1114112 | tf_op jit(solution)/shard_map/all_to_all | solution.py:290
  22.6 0.8 %reshape.38.halo_ref = s32[1,128]{1,0:T(1,128)S(1)} reshape(s32[1,2,64]{2,1,0:T(2,128)} %param.16) | data formatting | bytes 1024 | tf_op jit(solution)/shard_map/reshape | solution.py:354
  23.4 0.9 %copy_bitcast_fusion = (s32[27,512]{1,0:T(8,128)S(1)}, s32[27,512]{1,0:T(8,128)S(1)}) fusion(s32[1,27,512]{2,0,1:T(1,128)} %param.15, s32[1,27,512]{2,0,1:T(1,128)} %param.14), kind=kLoop, calls=%fused_computation | loop fusion | bytes 221184
  24.3 0.0 copy-start
  24.3 0.0 copy-start.1
  24.3 18.9 %rules.1 = (bf16[3,512,512]{2,1,0:T(8,128)(2,1)S(1)}, bf16[25,512,512]{2,1,0:T(8,128)(2,1)}, bf16[27,128,512]{2,1,0:T(8,128)(2,1)}) custom-call(s32[27,512]{1,0:T(8,128)S(1)} %get-tuple-element.20.rule_in_ref, s32[27,512]{1,0:T(8,128)S(1)} %get-tuple-element.19.rule_out_ref), custom_call_target="tpu_custom_call" | custom-call | flops 9059696640 | bytes 17694720 | tf_op jit(solution)/shard_map/rules/pallas_call | solution.py:294
  43.2 12.4 %all-to-all-done = bf16[64,17,2,128]{3,2,1,0:T(2,128)(2,1)S(1)} async-done(((bf16[64,17,2,128]{3,2,1,0:T(2,128)(2,1)}), bf16[64,17,2,128]{3,2,1,0:T(2,128)(2,1)S(1)}, u32[]{:S(2)}, u32[]{:S(2)}) %all-to-all-start) | async-done | bytes 557088 | tf_op jit(solution)/shard_map/all_to_all | solution.py:290
  55.6 0.0 copy-done
  55.6 0.0 copy-done.1
  55.6 4.5 %voxel.1 = (bf16[512,128]{1,0:T(8,128)(2,1)S(1)}, bf16[64,128]{1,0:T(8,128)(2,1)S(1)}, bf16[64,128]{1,0:T(8,128)(2,1)S(1)}, bf16[5120,512]{1,0:T(8,128)(2,1)S(1)}) custom-call(s32[1]{0:T(128)} %bitcast.me_ref, bf16[2176,128]{1,0:T(8,128)(2,1)S(1)} %bitcast.15, s32[17,128]{1,0:T(8,128)S(1)} %copy-done.1, bf16[3456,128]{1,0:T(8,128)(2,1)S(1)} %bitcast.13, ...), custom_call_target="tpu_custom_call" | custom-call | flops 452984832 | bytes 6000000 | tf_op jit(solution)/shard_map/voxel/pallas_call | solution.py:316
  60.1 2.9 %collective-permute-start = (bf16[64,128]{1,0:T(8,128)(2,1)S(1)}, bf16[64,128]{1,0:T(8,128)(2,1)S(1)}, u32[]{:S(2)}, u32[]{:S(2)}) collective-permute-start(bf16[64,128]{1,0:T(8,128)(2,1)S(1)} %get-tuple-element.17), channel_id=1, source_target_pairs={{0,1},{2,3},{4,5},{6,7},{8,9},{10,11},{12,13},{14,15},{16,17},{18,... | collective-permute-start | bytes 49160 | tf_op jit(solution)/shard_map/ppermute | solution.py:21
  63.0 3.4 %collective-permute-start.1 = (bf16[64,128]{1,0:T(8,128)(2,1)S(1)}, bf16[64,128]{1,0:T(8,128)(2,1)S(1)}, u32[]{:S(2)}, u32[]{:S(2)}) collective-permute-start(bf16[64,128]{1,0:T(8,128)(2,1)S(1)} %get-tuple-element.18), channel_id=1, source_target_pairs={{1,2},{3,4},{5,6},{7,8},{9,10},{11,12},{13,14},{15,16},{17,18},{19... | collective-permute-start | bytes 49160 | tf_op jit(solution)/shard_map/ppermute | solution.py:21
  66.4 0.0 copy-start.2
  66.5 3.9 %own.1.own_ref = f32[512,128]{1,0:T(8,128)S(1)} custom-call(bf16[1536,512]{1,0:T(8,128)(2,1)S(1)} %bitcast.16, bf16[5120,512]{1,0:T(8,128)(2,1)S(1)} %get-tuple-element.15.near_ref, bf16[12800,512]{1,0:T(8,128)(2,1)} %bitcast.19, bf16[512,128]{1,0:T(8,128)(2,1)S(1)} %get-tuple-element.16.voxels_ref, bf16[3456,128]{1,0:T(8,128)(2,1)S(1)} %bitcast.14), custom_call_target="tpu_custom_call" | custom-call | flops 2264924160 | bytes 14155776 | tf_op jit(solution)/shard_map/own/pallas_call | solution.py:335
  70.4 0.0 collective-permute-done.first_ref
  70.4 0.3 collective-permute-done.1.second_ref
  70.8 0.0 copy-done.2
  70.8 1.0 %final.1 = bf16[512,128]{1,0:T(8,128)(2,1)} custom-call(s32[1]{0:T(128)} %bitcast.me_ref, f32[512,128]{1,0:T(8,128)S(1)} %own.1.own_ref, bf16[512,128]{1,0:T(8,128)(2,1)S(1)} %get-tuple-element.16.voxels_ref, s32[1,128]{1,0:T(1,128)S(1)} %reshape.38.halo_ref, bf16[64,128]{1,0:T(8,128)(2,1)S(1)} %collective-permute-done.first_ref, ...), custom_call_target="tpu_custom_call" | custom-call | flops 16777216 | bytes 1000000 | tf_op jit(solution)/shard_map/final/pallas_call | solution.py:346
Async XLA Ops:
  3.8 51.8 %all-to-all-start = ((bf16[64,17,2,128]{3,2,1,0:T(2,128)(2,1)}), bf16[64,17,2,128]{3,2,1,0:T(2,128)(2,1)S(1)}, u32[]{:S(2)}, u32[]{:S(2)}) async-start(bf16[64,17,2,128]{3,2,1,0:T(2,128)(2,1)} %bitcast.21), calls=%async_computation | async-start | bytes 1114112 | tf_op jit(solution)/shard_map/all_to_all | solution.py:290
  24.3 31.4 %copy-start = (bf16[27,128,128]{2,1,0:T(8,128)(2,1)S(1)}, bf16[27,128,128]{2,1,0:T(8,128)(2,1)}, u32[]{:S(2)}) copy-start(bf16[27,128,128]{2,1,0:T(8,128)(2,1)} %param.12) | copy-start | bytes 2654212
  24.3 31.4 %copy-start.1 = (s32[17,128]{1,0:T(8,128)S(1)}, s32[17,128]{1,0:T(8,128)}, u32[]{:S(2)}) copy-start(s32[17,128]{1,0:T(8,128)} %constant.6.clone.class_ref) | copy-start | bytes 26116
  60.1 10.3 %collective-permute-start = (bf16[64,128]{1,0:T(8,128)(2,1)S(1)}, bf16[64,128]{1,0:T(8,128)(2,1)S(1)}, u32[]{:S(2)}, u32[]{:S(2)}) collective-permute-start(bf16[64,128]{1,0:T(8,128)(2,1)S(1)} %get-tuple-element.17), channel_id=1, source_target_pairs={{0,1},{2,3},{4,5},{6,7},{8,9},{10,11},{12,13},{14,15},{16,17},{18,... | collective-permute-start | bytes 49160 | tf_op jit(solution)/shard_map/ppermute | solution.py:21
  63.0 7.7 %collective-permute-start.1 = (bf16[64,128]{1,0:T(8,128)(2,1)S(1)}, bf16[64,128]{1,0:T(8,128)(2,1)S(1)}, u32[]{:S(2)}, u32[]{:S(2)}) collective-permute-start(bf16[64,128]{1,0:T(8,128)(2,1)S(1)} %get-tuple-element.18), channel_id=1, source_target_pairs={{1,2},{3,4},{5,6},{7,8},{9,10},{11,12},{13,14},{15,16},{17,18},{19... | collective-permute-start | bytes 49160 | tf_op jit(solution)/shard_map/ppermute | solution.py:21
  66.4 4.3 %copy-start.2 = (f32[128]{0:T(128)S(1)}, f32[128]{0:T(128)}, u32[]{:S(2)}) copy-start(f32[128]{0:T(128)} %param.13) | copy-start | bytes 1540

commit v5 on v4

--- a/solution.py
+++ b/solution.py
@@ -2,7 +2,6 @@
 
 import jax
 import jax.numpy as jnp
-import numpy as np
 from jax import lax
 from jax.experimental import pallas as pl
 from jax.experimental.pallas import tpu as pltpu
@@ -13,7 +12,7 @@
 BF = jnp.bfloat16
 F32 = jnp.float32
 PREP_MIB, RULES_MIB, VOXEL_MIB, OWN_MIB, FINAL_MIB = 16, 8, 16, 20, 4
-KEEP, NEAR, FAR_PARTS, PACK = 3, 10, 4, 256
+KEEP, NEAR, FAR_PARTS, PACK = 3, 6, 6, 256
 
 
 def exchanged(block, axis, first):
@@ -134,8 +133,8 @@
 
 
 def voxel_kernel(
-    bricks, cap, me_ref, arrived_ref, class_ref, conv_ref, edge_hbm, own_hbm,
-    voxels_ref, first_ref, second_ref, near_ref, edge_counts_ref, sems,
+    bricks, cap, me_ref, arrived_ref, conv_ref, edge_hbm, own_hbm,
+    voxels_ref, first_ref, second_ref, near_ref, wide_ref, edge_counts_ref, sems,
 ):
     near = near_ref.shape[0]
     copies = [
@@ -147,14 +146,11 @@
     for copy in copies:
         copy.start()
     per = cap + 2
-    chunks = class_ref.shape[0]
+    chunks = arrived_ref.shape[0] // LANES
     arrived = arrived_ref[...]
     numbers = row_iota(256)
-    pick = jnp.concatenate(
-        [one_hot_rows(numbers[: 2 * bricks], class_ref[c : c + 1, :], 0) for c in range(chunks)], axis=1
-    )
-    coded = dot(pick, arrived)
-    low, high = coded[:bricks], coded[bricks:]
+    wide_ref[...] = arrived.astype(F32)
+    low, high = (wide_ref[pl.ds(cap + i, bricks, stride=per), :] for i in range(2))
     begin = lax.broadcasted_iota(jnp.int32, (bricks, LANES), 0) * per
     lane = lax.broadcasted_iota(jnp.int32, (bricks, LANES), 1)
     stays = lane >= begin % LANES
@@ -260,10 +256,6 @@
     pairs = rule_in.shape[2]
     edges = 2 * halo_slots.shape[2]
     me = lax.axis_index("brick").astype(jnp.int32).reshape(1)
-    row_number = np.arange(rows)
-    brick_of, rank_of = row_number // per, row_number % per
-    classes = np.where(rank_of >= cap, (rank_of - cap) * bricks + brick_of, -1)
-    classes = jnp.asarray(classes.reshape(rows // LANES, LANES), jnp.int32)
     conv_rows = conv_weight.reshape(offsets * width, width)
     vmem = pl.BlockSpec(memory_space=pltpu.VMEM)
     hbm = pl.BlockSpec(memory_space=pl.ANY)
@@ -321,13 +313,17 @@
             jax.ShapeDtypeStruct((edges // 2, width), BF),
             pltpu.VMEM((near, VOX), BF),
         ),
-        in_specs=[smem] + [vmem] * 3 + [hbm] * 2,
+        in_specs=[smem] + [vmem] * 2 + [hbm] * 2,
         out_specs=(vmem,) * 4,
-        scratch_shapes=[pltpu.VMEM((offsets * edges, VOX), BF), pltpu.SemaphoreType.DMA((2,))],
+        scratch_shapes=[
+            pltpu.VMEM((rows, width), F32),
+            pltpu.VMEM((offsets * edges, VOX), BF),
+            pltpu.SemaphoreType.DMA((2,)),
+        ],
         compiler_params=params(VOXEL_MIB),
         cost_estimate=cost(2 * offsets * edges * VOX * width, 6_000_000),
         name="voxel",
-    )(me, arrived, classes, conv_rows, edge_counts, own_counts)
+    )(me, arrived, conv_rows, edge_counts, own_counts)
 
     from_first = exchanged(first, "brick", 0)
     from_second = exchanged(second, "brick", 1)

time: 72 us -> 71.9 us (level)
  local copies, waits for them, and re-layouts: 1.63 us -> 0.79 us
    unnamed x7 -> x9, local copies, waits for them, and re-layouts: 0.87 us -> 0.03 us
    all_to_all x1, waiting for transfers between devices: 12.4 us -> 13.2 us  [per_device(): lax.all_to_all(send.reshape(bricks, per // 2, 2, width), 'brick', split_a...]
  transfers between devices with their start and end apart: 3 -> 3, of which waited for: 2 -> 1; matrix products, arithmetic and copies ran while one was open for 2% -> 1% of each run, Pallas kernels for 32% -> 33%
where the time goes in v5:
time: 71.9 us; the launch traced here: 71.6 us
  Pallas kernels  32.5 us (45%)
  starting transfers between devices  25.1 us (35%)
  waiting for transfers between devices  13.2 us (18%)
  local copies, waits for them, and re-layouts  0.79 us (1%)
    pallas_call x1, Pallas kernels, per_device(): pl.pallas_call(rules_kernel, out_shape=(pltpu.VMEM((KEEP, VOX, VOX), BF),...  19 us
    all_to_all x1, starting transfers between devices, per_device(): lax.all_to_all(send.reshape(bricks, per // 2, 2, width), 'brick', split_a...  18.8 us
    all_to_all x1, waiting for transfers between devices, per_device(): lax.all_to_all(send.reshape(bricks, per // 2, 2, width), 'brick', split_a...  13.2 us
    ppermute x2, starting transfers between devices, exchanged(): return lax.ppermute(block, axis, pairs + [(b, a) for a, b in pairs])  6.27 us
    pallas_call x1, Pallas kernels, per_device(): pl.pallas_call(own_kernel, out_shape=jax.ShapeDtypeStruct((VOX, width), F...  4.5 us
    pallas_call x1, Pallas kernels, per_device(): pl.pallas_call(functools.partial(voxel_kernel, bricks, cap), out_shape=(j...  4.17 us
    pallas_call x1, Pallas kernels, per_device(): pl.pallas_call(functools.partial(prep_kernel, bricks, cap), out_shape=plt...  3.84 us
  transfers between devices with their start and end apart: 3, of which 1 were waited for; matrix products, arithmetic and copies ran while one was open for 1% of the time, Pallas kernels for 33%

profile of v5, /device:TPU:6, one launch (start us, length us, event | category | flops | bytes accessed | tf_op | source)
XLA Modules:
  0.0 71.6 jit_solution(9726602560529232688)
XLA Ops:
  0.0 0.0 copy-start.2
  0.0 0.0 copy-start.3
  0.0 3.8 %prep.1 = bf16[2176,128]{1,0:T(8,128)(2,1)} custom-call(s32[1]{0:T(128)} %bitcast.me_ref, s32[8,128]{1,0:T(8,128)} %bitcast.22, bf16[1024,384]{1,0:T(8,128)(2,1)} %tokens_hbm.1, bf16[384,128]{1,0:T(8,128)(2,1)} %weight_hbm.1), custom_call_target="tpu_custom_call" | custom-call | flops 641728512 | bytes 2000000 | tf_op jit(solution)/shard_map/prep/pallas_call | solution.py:264
  3.9 18.8 %all-to-all-start = ((bf16[64,17,2,128]{3,2,1,0:T(2,128)(2,1)}), bf16[64,17,2,128]{3,2,1,0:T(2,128)(2,1)S(1)}, u32[]{:S(2)}, u32[]{:S(2)}) async-start(bf16[64,17,2,128]{3,2,1,0:T(2,128)(2,1)} %bitcast.21), calls=%async_computation | async-start | bytes 1114112 | tf_op jit(solution)/shard_map/all_to_all | solution.py:282
  22.7 0.8 %reshape.38.halo_ref = s32[1,128]{1,0:T(1,128)S(1)} reshape(s32[1,2,64]{2,1,0:T(2,128)} %param.15) | data formatting | bytes 1024 | tf_op jit(solution)/shard_map/reshape | solution.py:350
  23.4 0.0 copy-done.2
  23.4 0.0 copy-done.3
  23.4 0.0 copy-start
  23.5 19.0 %rules.1 = (bf16[3,512,512]{2,1,0:T(8,128)(2,1)S(1)}, bf16[25,512,512]{2,1,0:T(8,128)(2,1)}, bf16[27,128,512]{2,1,0:T(8,128)(2,1)}) custom-call(s32[27,512]{1,0:T(8,128)S(1)} %get-tuple-element.20.rule_in_ref, s32[27,512]{1,0:T(8,128)S(1)} %get-tuple-element.19.rule_out_ref), custom_call_target="tpu_custom_call" | custom-call | flops 9059696640 | bytes 17694720 | tf_op jit(solution)/shard_map/rules/pallas_call | solution.py:286
  42.4 13.2 %all-to-all-done = bf16[64,17,2,128]{3,2,1,0:T(2,128)(2,1)S(1)} async-done(((bf16[64,17,2,128]{3,2,1,0:T(2,128)(2,1)}), bf16[64,17,2,128]{3,2,1,0:T(2,128)(2,1)S(1)}, u32[]{:S(2)}, u32[]{:S(2)}) %all-to-all-start) | async-done | bytes 557088 | tf_op jit(solution)/shard_map/all_to_all | solution.py:282
  55.7 0.0 copy-done
  55.7 4.2 %voxel.1 = (bf16[512,128]{1,0:T(8,128)(2,1)S(1)}, bf16[64,128]{1,0:T(8,128)(2,1)S(1)}, bf16[64,128]{1,0:T(8,128)(2,1)S(1)}, bf16[3072,512]{1,0:T(8,128)(2,1)S(1)}) custom-call(s32[1]{0:T(128)} %bitcast.me_ref, bf16[2176,128]{1,0:T(8,128)(2,1)S(1)} %bitcast.15, bf16[3456,128]{1,0:T(8,128)(2,1)S(1)} %bitcast.13, bf16[3456,512]{1,0:T(8,128)(2,1)} %bitcast.20, ...), custom_call_target="tpu_custom_call" | custom-call | flops 452984832 | bytes 6000000 | tf_op jit(solution)/shard_map/voxel/pallas_call | solution.py:308
  59.8 2.9 %collective-permute-start = (bf16[64,128]{1,0:T(8,128)(2,1)S(1)}, bf16[64,128]{1,0:T(8,128)(2,1)S(1)}, u32[]{:S(2)}, u32[]{:S(2)}) collective-permute-start(bf16[64,128]{1,0:T(8,128)(2,1)S(1)} %get-tuple-element.17), channel_id=1, source_target_pairs={{0,1},{2,3},{4,5},{6,7},{8,9},{10,11},{12,13},{14,15},{16,17},{18,... | collective-permute-start | bytes 49160 | tf_op jit(solution)/shard_map/ppermute | solution.py:20
  62.7 3.4 %collective-permute-start.1 = (bf16[64,128]{1,0:T(8,128)(2,1)S(1)}, bf16[64,128]{1,0:T(8,128)(2,1)S(1)}, u32[]{:S(2)}, u32[]{:S(2)}) collective-permute-start(bf16[64,128]{1,0:T(8,128)(2,1)S(1)} %get-tuple-element.18), channel_id=1, source_target_pairs={{1,2},{3,4},{5,6},{7,8},{9,10},{11,12},{13,14},{15,16},{17,18},{19... | collective-permute-start | bytes 49160 | tf_op jit(solution)/shard_map/ppermute | solution.py:20
  66.1 0.0 copy-start.1
  66.1 4.5 %own.1.own_ref = f32[512,128]{1,0:T(8,128)S(1)} custom-call(bf16[1536,512]{1,0:T(8,128)(2,1)S(1)} %bitcast.16, bf16[3072,512]{1,0:T(8,128)(2,1)S(1)} %get-tuple-element.15.near_ref, bf16[12800,512]{1,0:T(8,128)(2,1)} %bitcast.19, bf16[512,128]{1,0:T(8,128)(2,1)S(1)} %get-tuple-element.16.voxels_ref, bf16[3456,128]{1,0:T(8,128)(2,1)S(1)} %bitcast.14), custom_call_target="tpu_custom_call" | custom-call | flops 2264924160 | bytes 14155776 | tf_op jit(solution)/shard_map/own/pallas_call | solution.py:331
  70.6 0.0 collective-permute-done.first_ref
  70.6 0.0 collective-permute-done.1.second_ref
  70.7 0.0 copy-done.1
  70.7 1.0 %final.1 = bf16[512,128]{1,0:T(8,128)(2,1)} custom-call(s32[1]{0:T(128)} %bitcast.me_ref, f32[512,128]{1,0:T(8,128)S(1)} %own.1.own_ref, bf16[512,128]{1,0:T(8,128)(2,1)S(1)} %get-tuple-element.16.voxels_ref, s32[1,128]{1,0:T(1,128)S(1)} %reshape.38.halo_ref, bf16[64,128]{1,0:T(8,128)(2,1)S(1)} %collective-permute-done.first_ref, ...), custom_call_target="tpu_custom_call" | custom-call | flops 16777216 | bytes 1000000 | tf_op jit(solution)/shard_map/final/pallas_call | solution.py:342
  (1 shorter events, 0.0 us)
Async XLA Ops:
  0.0 23.4 %copy-start.2 = (s32[1,27,512]{2,0,1:T(1,128)S(1)}, s32[1,27,512]{2,0,1:T(1,128)}, u32[]{:S(2)}) copy-start(s32[1,27,512]{2,0,1:T(1,128)} %param.14) | copy-start | bytes 165892
  0.0 23.4 %copy-start.3 = (s32[1,27,512]{2,0,1:T(1,128)S(1)}, s32[1,27,512]{2,0,1:T(1,128)}, u32[]{:S(2)}) copy-start(s32[1,27,512]{2,0,1:T(1,128)} %param.13) | copy-start | bytes 165892
  3.9 51.8 %all-to-all-start = ((bf16[64,17,2,128]{3,2,1,0:T(2,128)(2,1)}), bf16[64,17,2,128]{3,2,1,0:T(2,128)(2,1)S(1)}, u32[]{:S(2)}, u32[]{:S(2)}) async-start(bf16[64,17,2,128]{3,2,1,0:T(2,128)(2,1)} %bitcast.21), calls=%async_computation | async-start | bytes 1114112 | tf_op jit(solution)/shard_map/all_to_all | solution.py:282
  23.4 32.2 %copy-start = (bf16[27,128,128]{2,1,0:T(8,128)(2,1)S(1)}, bf16[27,128,128]{2,1,0:T(8,128)(2,1)}, u32[]{:S(2)}) copy-start(bf16[27,128,128]{2,1,0:T(8,128)(2,1)} %param.11) | copy-start | bytes 2654212
  59.8 10.8 %collective-permute-start = (bf16[64,128]{1,0:T(8,128)(2,1)S(1)}, bf16[64,128]{1,0:T(8,128)(2,1)S(1)}, u32[]{:S(2)}, u32[]{:S(2)}) collective-permute-start(bf16[64,128]{1,0:T(8,128)(2,1)S(1)} %get-tuple-element.17), channel_id=1, source_target_pairs={{0,1},{2,3},{4,5},{6,7},{8,9},{10,11},{12,13},{14,15},{16,17},{18,... | collective-permute-start | bytes 49160 | tf_op jit(solution)/shard_map/ppermute | solution.py:20
  62.7 8.0 %collective-permute-start.1 = (bf16[64,128]{1,0:T(8,128)(2,1)S(1)}, bf16[64,128]{1,0:T(8,128)(2,1)S(1)}, u32[]{:S(2)}, u32[]{:S(2)}) collective-permute-start(bf16[64,128]{1,0:T(8,128)(2,1)S(1)} %get-tuple-element.18), channel_id=1, source_target_pairs={{1,2},{3,4},{5,6},{7,8},{9,10},{11,12},{13,14},{15,16},{17,18},{19... | collective-permute-start | bytes 49160 | tf_op jit(solution)/shard_map/ppermute | solution.py:20
  66.1 4.5 %copy-start.1 = (f32[128]{0:T(128)S(1)}, f32[128]{0:T(128)}, u32[]{:S(2)}) copy-start(f32[128]{0:T(128)} %param.12) | copy-start | bytes 1540

commit v6 on v5

--- a/solution.py
+++ b/solution.py
@@ -12,7 +12,7 @@
 BF = jnp.bfloat16
 F32 = jnp.float32
 PREP_MIB, RULES_MIB, VOXEL_MIB, OWN_MIB, FINAL_MIB = 16, 8, 16, 20, 4
-KEEP, NEAR, FAR_PARTS, PACK = 3, 6, 6, 256
+KEEP, NEAR, FAR_PARTS, PACK = 4, 9, 4, 256
 
 
 def exchanged(block, axis, first):

time: 71.9 us -> 71.7 us (level)
  Pallas kernels: 32.5 us -> 31.6 us
  local copies, waits for them, and re-layouts: 0.79 us -> 1.63 us
    unnamed x9 -> x5, local copies, waits for them, and re-layouts: 0.03 us -> 0.86 us
    pallas_call x1, Pallas kernels: 4.5 us -> 3.7 us  [per_device(): pl.pallas_call(own_kernel, out_shape=jax.ShapeDtypeStruct((VOX, width), F...]
    all_to_all x1, waiting for transfers between devices: 13.2 us -> 12.5 us  [per_device(): lax.all_to_all(send.reshape(bricks, per // 2, 2, width), 'brick', split_a...]
  transfers between devices with their start and end apart: 3 -> 3, of which waited for: 1 -> 2; matrix products, arithmetic and copies ran while one was open for 1% -> 2% of each run, Pallas kernels for 33% -> 32%
where the time goes in v6:
time: 71.7 us; the launch traced here: 71.4 us
  Pallas kernels  31.6 us (44%)
  starting transfers between devices  25.1 us (35%)
  waiting for transfers between devices  13 us (18%)
  local copies, waits for them, and re-layouts  1.63 us (2%)
    pallas_call x1, Pallas kernels, per_device(): pl.pallas_call(rules_kernel, out_shape=(pltpu.VMEM((KEEP, VOX, VOX), BF),...  18.9 us
    all_to_all x1, starting transfers between devices, per_device(): lax.all_to_all(send.reshape(bricks, per // 2, 2, width), 'brick', split_a...  18.8 us
    all_to_all x1, waiting for transfers between devices, per_device(): lax.all_to_all(send.reshape(bricks, per // 2, 2, width), 'brick', split_a...  12.5 us
    ppermute x2, starting transfers between devices, exchanged(): return lax.ppermute(block, axis, pairs + [(b, a) for a, b in pairs])  6.29 us
    pallas_call x1, Pallas kernels, per_device(): pl.pallas_call(functools.partial(voxel_kernel, bricks, cap), out_shape=(j...  4.17 us
    pallas_call x1, Pallas kernels, per_device(): pl.pallas_call(functools.partial(prep_kernel, bricks, cap), out_shape=plt...  3.83 us
    pallas_call x1, Pallas kernels, per_device(): pl.pallas_call(own_kernel, out_shape=jax.ShapeDtypeStruct((VOX, width), F...  3.7 us
  transfers between devices with their start and end apart: 3, of which 2 were waited for; matrix products, arithmetic and copies ran while one was open for 2% of the time, Pallas kernels for 32%

profile of v6, /device:TPU:6, one launch (start us, length us, event | category | flops | bytes accessed | tf_op | source)
XLA Modules:
  0.0 71.4 jit_solution(10368410734908358747)
XLA Ops:
  0.0 3.8 %prep.1 = bf16[2176,128]{1,0:T(8,128)(2,1)} custom-call(s32[1]{0:T(128)} %bitcast.me_ref, s32[8,128]{1,0:T(8,128)} %bitcast.22, bf16[1024,384]{1,0:T(8,128)(2,1)} %tokens_hbm.1, bf16[384,128]{1,0:T(8,128)(2,1)} %weight_hbm.1), custom_call_target="tpu_custom_call" | custom-call | flops 641728512 | bytes 2000000 | tf_op jit(solution)/shard_map/prep/pallas_call | solution.py:264
  3.8 18.8 %all-to-all-start = ((bf16[64,17,2,128]{3,2,1,0:T(2,128)(2,1)}), bf16[64,17,2,128]{3,2,1,0:T(2,128)(2,1)S(1)}, u32[]{:S(2)}, u32[]{:S(2)}) async-start(bf16[64,17,2,128]{3,2,1,0:T(2,128)(2,1)} %bitcast.21), calls=%async_computation | async-start | bytes 1114112 | tf_op jit(solution)/shard_map/all_to_all | solution.py:282
  22.7 0.8 %reshape.38.halo_ref = s32[1,128]{1,0:T(1,128)S(1)} reshape(s32[1,2,64]{2,1,0:T(2,128)} %param.15) | data formatting | bytes 1024 | tf_op jit(solution)/shard_map/reshape | solution.py:350
  23.4 0.9 %copy_bitcast_fusion = (s32[27,512]{1,0:T(8,128)S(1)}, s32[27,512]{1,0:T(8,128)S(1)}) fusion(s32[1,27,512]{2,0,1:T(1,128)} %param.14, s32[1,27,512]{2,0,1:T(1,128)} %param.13), kind=kLoop, calls=%fused_computation | loop fusion | bytes 221184
  24.3 0.0 copy-start
  24.3 18.9 %rules.1 = (bf16[4,512,512]{2,1,0:T(8,128)(2,1)S(1)}, bf16[24,512,512]{2,1,0:T(8,128)(2,1)}, bf16[27,128,512]{2,1,0:T(8,128)(2,1)}) custom-call(s32[27,512]{1,0:T(8,128)S(1)} %get-tuple-element.20.rule_in_ref, s32[27,512]{1,0:T(8,128)S(1)} %get-tuple-element.19.rule_out_ref), custom_call_target="tpu_custom_call" | custom-call | flops 9059696640 | bytes 17694720 | tf_op jit(solution)/shard_map/rules/pallas_call | solution.py:286
  43.2 12.5 %all-to-all-done = bf16[64,17,2,128]{3,2,1,0:T(2,128)(2,1)S(1)} async-done(((bf16[64,17,2,128]{3,2,1,0:T(2,128)(2,1)}), bf16[64,17,2,128]{3,2,1,0:T(2,128)(2,1)S(1)}, u32[]{:S(2)}, u32[]{:S(2)}) %all-to-all-start) | async-done | bytes 557088 | tf_op jit(solution)/shard_map/all_to_all | solution.py:282
  55.6 0.0 copy-done
  55.6 4.2 %voxel.1 = (bf16[512,128]{1,0:T(8,128)(2,1)S(1)}, bf16[64,128]{1,0:T(8,128)(2,1)S(1)}, bf16[64,128]{1,0:T(8,128)(2,1)S(1)}, bf16[4608,512]{1,0:T(8,128)(2,1)S(1)}) custom-call(s32[1]{0:T(128)} %bitcast.me_ref, bf16[2176,128]{1,0:T(8,128)(2,1)S(1)} %bitcast.15, bf16[3456,128]{1,0:T(8,128)(2,1)S(1)} %bitcast.13, bf16[3456,512]{1,0:T(8,128)(2,1)} %bitcast.20, ...), custom_call_target="tpu_custom_call" | custom-call | flops 452984832 | bytes 6000000 | tf_op jit(solution)/shard_map/voxel/pallas_call | solution.py:308
  59.8 2.9 %collective-permute-start = (bf16[64,128]{1,0:T(8,128)(2,1)S(1)}, bf16[64,128]{1,0:T(8,128)(2,1)S(1)}, u32[]{:S(2)}, u32[]{:S(2)}) collective-permute-start(bf16[64,128]{1,0:T(8,128)(2,1)S(1)} %get-tuple-element.17), channel_id=1, source_target_pairs={{0,1},{2,3},{4,5},{6,7},{8,9},{10,11},{12,13},{14,15},{16,17},{18,... | collective-permute-start | bytes 49160 | tf_op jit(solution)/shard_map/ppermute | solution.py:20
  62.7 3.4 %collective-permute-start.1 = (bf16[64,128]{1,0:T(8,128)(2,1)S(1)}, bf16[64,128]{1,0:T(8,128)(2,1)S(1)}, u32[]{:S(2)}, u32[]{:S(2)}) collective-permute-start(bf16[64,128]{1,0:T(8,128)(2,1)S(1)} %get-tuple-element.18), channel_id=1, source_target_pairs={{1,2},{3,4},{5,6},{7,8},{9,10},{11,12},{13,14},{15,16},{17,18},{19... | collective-permute-start | bytes 49160 | tf_op jit(solution)/shard_map/ppermute | solution.py:20
  66.1 0.0 copy-start.1
  66.1 3.7 %own.1.own_ref = f32[512,128]{1,0:T(8,128)S(1)} custom-call(bf16[2048,512]{1,0:T(8,128)(2,1)S(1)} %bitcast.16, bf16[4608,512]{1,0:T(8,128)(2,1)S(1)} %get-tuple-element.15.near_ref, bf16[12288,512]{1,0:T(8,128)(2,1)} %bitcast.19, bf16[512,128]{1,0:T(8,128)(2,1)S(1)} %get-tuple-element.16.voxels_ref, bf16[3456,128]{1,0:T(8,128)(2,1)S(1)} %bitcast.14), custom_call_target="tpu_custom_call" | custom-call | flops 2264924160 | bytes 14155776 | tf_op jit(solution)/shard_map/own/pallas_call | solution.py:331
  69.9 0.0 collective-permute-done.first_ref
  69.9 0.6 collective-permute-done.1.second_ref
  70.4 0.0 copy-done.1
  70.4 1.0 %final.1 = bf16[512,128]{1,0:T(8,128)(2,1)} custom-call(s32[1]{0:T(128)} %bitcast.me_ref, f32[512,128]{1,0:T(8,128)S(1)} %own.1.own_ref, bf16[512,128]{1,0:T(8,128)(2,1)S(1)} %get-tuple-element.16.voxels_ref, s32[1,128]{1,0:T(1,128)S(1)} %reshape.38.halo_ref, bf16[64,128]{1,0:T(8,128)(2,1)S(1)} %collective-permute-done.first_ref, ...), custom_call_target="tpu_custom_call" | custom-call | flops 16777216 | bytes 1000000 | tf_op jit(solution)/shard_map/final/pallas_call | solution.py:342
Async XLA Ops:
  3.8 51.8 %all-to-all-start = ((bf16[64,17,2,128]{3,2,1,0:T(2,128)(2,1)}), bf16[64,17,2,128]{3,2,1,0:T(2,128)(2,1)S(1)}, u32[]{:S(2)}, u32[]{:S(2)}) async-start(bf16[64,17,2,128]{3,2,1,0:T(2,128)(2,1)} %bitcast.21), calls=%async_computation | async-start | bytes 1114112 | tf_op jit(solution)/shard_map/all_to_all | solution.py:282
  24.3 31.4 %copy-start = (bf16[27,128,128]{2,1,0:T(8,128)(2,1)S(1)}, bf16[27,128,128]{2,1,0:T(8,128)(2,1)}, u32[]{:S(2)}) copy-start(bf16[27,128,128]{2,1,0:T(8,128)(2,1)} %param.11) | copy-start | bytes 2654212
  59.8 10.0 %collective-permute-start = (bf16[64,128]{1,0:T(8,128)(2,1)S(1)}, bf16[64,128]{1,0:T(8,128)(2,1)S(1)}, u32[]{:S(2)}, u32[]{:S(2)}) collective-permute-start(bf16[64,128]{1,0:T(8,128)(2,1)S(1)} %get-tuple-element.17), channel_id=1, source_target_pairs={{0,1},{2,3},{4,5},{6,7},{8,9},{10,11},{12,13},{14,15},{16,17},{18,... | collective-permute-start | bytes 49160 | tf_op jit(solution)/shard_map/ppermute | solution.py:20
  62.7 7.7 %collective-permute-start.1 = (bf16[64,128]{1,0:T(8,128)(2,1)S(1)}, bf16[64,128]{1,0:T(8,128)(2,1)S(1)}, u32[]{:S(2)}, u32[]{:S(2)}) collective-permute-start(bf16[64,128]{1,0:T(8,128)(2,1)S(1)} %get-tuple-element.18), channel_id=1, source_target_pairs={{1,2},{3,4},{5,6},{7,8},{9,10},{11,12},{13,14},{15,16},{17,18},{19... | collective-permute-start | bytes 49160 | tf_op jit(solution)/shard_map/ppermute | solution.py:20
  66.1 4.3 %copy-start.1 = (f32[128]{0:T(128)S(1)}, f32[128]{0:T(128)}, u32[]{:S(2)}) copy-start(f32[128]{0:T(128)} %param.12) | copy-start | bytes 1540
